TPU v7x, 512 devices: a whole 4x4x16 slice. The times are simulated.
512 devices in a mesh: sec: 8 (over x, core), row: 8 (over y, z_hi), col: 8 (over z_lo).
Axes of the slice: x: 4, y: 4, z: 16 (z_hi: 2, z_lo: 8; z = z_hi * 8 + z_lo), core: 2. Of those that a mesh axis runs over, the one named last changes fastest.
Arguments:
- images: float32 [16, 3072, 3072], P('sec', 'row', 'col'), may hold values from -18 to 18
- offsets: int32 [2, 16, 24, 24], P(None, 'sec', 'row', 'col'), may hold values from -64 to 64
- warp: float32 [2, 16, 24, 24], P(None, 'sec', 'row', 'col'), may hold values from -2 to 2
- stiffness: float32 [2, 16, 24, 24], P(None, 'sec', 'row', 'col'), may hold values from 0.04 to 0.25
- valid: int32 [16, 24, 24], P('sec', 'row', 'col'), may hold values 0 or 1
Outputs:
- displacement: float32 [2, 16, 24, 24], P(None, 'sec', 'row', 'col')
- warped: float32 [2, 16, 24, 24], P(None, 'sec', 'row', 'col')
All inputs are finite; a program needn't handle non-finite values. No bound on the sum of `valid` on one device may be relied on, other than what follows from the above.
Results may differ from a plain program's by a relative error of at most 0.0003.
Values sent between devices are 32-bit elements; how exact they have to be, the bound alone decides.
A program may use at most 64 MiB of HBM per device.

v0:
```python
import jax
import jax.numpy as jnp
from jax import lax
from jax.sharding import PartitionSpec as P

P_SIZE = 128
MAXOFF = 64
ITERS = 3


SHARPNESS = 80.0
ANCHOR_STIFFNESS = 0.2


def extended(shard, sides, width):
    for axis, dim in sides:
        peers, length = (lax.axis_size(axis), shard.shape[dim])
        up = [(i, (i + 1) % peers) for i in range(peers - 1)]
        down = [(j, i) for i, j in up]
        last = lax.slice_in_dim(shard, length - width, length, axis=dim)
        first = lax.slice_in_dim(shard, 0, width, axis=dim)
        before = lax.ppermute(last, axis, up)
        after = lax.ppermute(first, axis, down)
        shard = jnp.concatenate([before, shard, after], axis=dim)
    return shard


def shifted(block, axis, distance):
    devices = range(lax.axis_size(axis))
    route = [(i - distance, i) for i in devices if i - distance in devices]
    return lax.ppermute(block, axis, route)


def prefix(shard, axis, combine, identity):
    peers, position = (lax.axis_size(axis), lax.axis_index(axis))
    everything = lax.all_gather(shard, axis)
    start = jnp.broadcast_to(jnp.asarray(identity, shard.dtype), shard.shape)

    def lap(k, before):
        reached = k < position
        new = combine(before, everything[k])
        return jnp.where(reached, new, before)

    return lax.fori_loop(0, peers, lap, start)


def tables():
    index = jnp.arange(P_SIZE, dtype=jnp.int32)
    phase = index[:, None] * index[None, :] % P_SIZE
    angles = phase.astype(jnp.float32) * (2.0 * jnp.pi / P_SIZE)
    return (jnp.cos(angles), jnp.sin(angles))


def expectation(scores):
    half_side = P_SIZE // 2
    coords = ((jnp.arange(P_SIZE, dtype=jnp.int32) + half_side) % P_SIZE - half_side).astype(
        jnp.float32
    )
    highest = jnp.max(scores, axis=(1, 2), keepdims=True)
    weights = jnp.exp(scores - highest)
    total = jnp.sum(weights, axis=(1, 2))
    along_rows = jnp.sum(weights * coords[None, :, None], axis=(1, 2)) / total
    along_cols = jnp.sum(weights * coords[None, None, :], axis=(1, 2)) / total
    return (along_rows, along_cols)


def right_mul(blocks, table):
    return jnp.einsum("nyx,xk->nyk", blocks, table, precision=lax.Precision.HIGHEST)


def left_mul(table, blocks):
    return jnp.einsum("jy,nyk->njk", table, blocks, precision=lax.Precision.HIGHEST)


def spectrum(blocks, cosine, sine):
    with_cos = right_mul(blocks, cosine)
    with_sin = right_mul(blocks, sine)
    real_part = left_mul(cosine, with_cos) - left_mul(sine, with_sin)
    imag_part = -(left_mul(cosine, with_sin) + left_mul(sine, with_cos))
    return (real_part, imag_part)


def soft_peak(mine, theirs, cosine, sine):
    mine = mine - jnp.mean(mine, axis=(1, 2), keepdims=True)
    theirs = theirs - jnp.mean(theirs, axis=(1, 2), keepdims=True)
    mine_real, mine_imag = spectrum(mine, cosine, sine)
    their_real, their_imag = spectrum(theirs, cosine, sine)
    cross_real = mine_real * their_real + mine_imag * their_imag
    cross_imag = mine_real * their_imag - mine_imag * their_real
    first_half = right_mul(cross_real, cosine) - right_mul(cross_imag, sine)
    second_half = right_mul(cross_real, sine) + right_mul(cross_imag, cosine)
    correlation = (left_mul(cosine, first_half) - left_mul(sine, second_half)) * (
        1.0 / (P_SIZE * P_SIZE)
    )
    scores = correlation * (SHARPNESS / (P_SIZE * P_SIZE))
    return expectation(scores)


def pull(
    current,
    right_nb,
    left_nb,
    down_nb,
    upper_nb,
    right,
    right_left,
    down,
    down_upper,
    anchor,
    target,
):
    return (
        current
        + right * (right_nb - current)
        + right_left * (left_nb - current)
        + down * (down_nb - current)
        + down_upper * (upper_nb - current)
        + anchor * (target - current)
    )


def per_device(images, offsets, warp, stiffness, valid):
    sections = images.shape[0]
    per_side = offsets.shape[2]
    cosine, sine = tables()
    rimmed = extended(images, (("row", 1), ("col", 2)), MAXOFF)
    arriving = shifted(rimmed[0:1], "sec", -1)
    upcoming = jnp.concatenate([rimmed[1:], arriving], 0)
    own = images.reshape(sections, per_side, P_SIZE, per_side, P_SIZE).transpose(0, 1, 3, 2, 4)
    own = own.reshape(sections, per_side * per_side, P_SIZE, P_SIZE)
    grid_start = jnp.arange(per_side, dtype=jnp.int32) * P_SIZE
    starts_row = (MAXOFF + grid_start[:, None] + offsets[0]).reshape(sections, per_side * per_side)
    starts_col = (MAXOFF + grid_start[None, :] + offsets[1]).reshape(sections, per_side * per_side)

    def cut_section(frame, rows_at, cols_at):
        return jax.vmap(
            lambda start_row, start_col: lax.dynamic_slice(
                frame, (start_row, start_col), (P_SIZE, P_SIZE)
            )
        )(rows_at, cols_at)

    theirs = jax.vmap(cut_section)(upcoming, starts_row, starts_col)

    def section_peak(packed):
        return soft_peak(packed[0], packed[1], cosine, sine)

    along_rows, along_cols = lax.map(section_peak, (own, theirs))
    peaks = jnp.stack([along_rows, along_cols]).reshape(2, sections, per_side, per_side)
    displacement = (offsets.astype(jnp.float32) + peaks) / P_SIZE
    final_device = lax.axis_index("sec") == lax.axis_size("sec") - 1
    silent = final_device & (jnp.arange(sections) == sections - 1)
    displacement = jnp.where(
        silent[None, :, None, None], jnp.zeros_like(displacement), displacement
    )
    local_before = jnp.cumsum(displacement, axis=1) - displacement
    totals = jnp.sum(displacement, axis=1)
    earlier = prefix(
        totals,
        "sec",
        lambda earlier_part, later_part: earlier_part + later_part,
        jnp.zeros_like(totals),
    )
    target = warp - (earlier[:, None] + local_before)
    position = jnp.arange(per_side)
    last_col = (lax.axis_index("col") == lax.axis_size("col") - 1) & (position == per_side - 1)
    last_row = (lax.axis_index("row") == lax.axis_size("row") - 1) & (position == per_side - 1)
    right = jnp.where(last_col[None, None, :], 0.0, stiffness[0])
    down = jnp.where(last_row[None, :, None], 0.0, stiffness[1])
    anchor = ANCHOR_STIFFNESS * valid.astype(jnp.float32)
    left_edge = shifted(right[:, :, -1:], "col", 1)
    upper_edge = shifted(down[:, -1:, :], "row", 1)
    right_left = jnp.concatenate([left_edge, right[:, :, :-1]], 2)
    down_upper = jnp.concatenate([upper_edge, down[:, :-1, :]], 1)
    warped = warp
    for iteration in range(ITERS):
        padded = extended(warped, (("row", 2), ("col", 3)), 1)
        warped = pull(
            warped,
            padded[:, :, 1:-1, 2:],
            padded[:, :, 1:-1, :-2],
            padded[:, :, 2:, 1:-1],
            padded[:, :, :-2, 1:-1],
            right,
            right_left,
            down,
            down_upper,
            anchor,
            target,
        )
    return (displacement, warped)


def solution(mesh):
    return jax.shard_map(
        per_device,
        mesh=mesh,
        in_specs=(
            P("sec", "row", "col"),
            P(None, "sec", "row", "col"),
            P(None, "sec", "row", "col"),
            P(None, "sec", "row", "col"),
            P("sec", "row", "col"),
        ),
        out_specs=(P(None, "sec", "row", "col"), P(None, "sec", "row", "col")),
        check_vma=False,
    )
```

profile of v0, /device:TPU:6, one launch (start us, length us, event | category | flops | bytes accessed | tf_op | source)
XLA Modules:
  0.0 287.0 jit_solution(5157677066162930275)
XLA Ops:
  2.4 16.5 %collective-permute-start = (f32[2,64,384]{2,1,0:T(8,128)}, f32[2,64,384]{2,1,0:T(8,128)}, u32[]{:S(2)}, u32[]{:S(2)}) collective-permute-start(f32[2,64,384]{2,1,0:T(8,128)} %get-tuple-element.369), channel_id=1, source_target_pairs={{0,8},{8,16},{16,24},{24,32},{32,40},{40,48},{48,56},{1,9},{9,17},... | collective-permute-start | bytes 589832 | tf_op jit(solution)/shard_map/ppermute | solution.py:22
  21.5 13.8 %collective-permute-start.5 = (f32[2,2,1,3]{3,2,1,0:T(1,128)}, f32[2,2,1,3]{3,2,1,0:T(1,128)}, u32[]{:S(2)}, u32[]{:S(2)}) collective-permute-start(f32[2,2,1,3]{3,2,1,0:T(1,128)} %bitcast.4), channel_id=1, source_target_pairs={{0,8},{8,16},{16,24},{24,32},{32,40},{40,48},{48,56},{1,9},{9,17},... | collective-permute-start | bytes 152 | tf_op jit(solution)/shard_map/ppermute | solution.py:22
  37.9 13.8 %collective-permute-start.10 = (f32[2,1,3]{2,0,1:T(2,128)}, f32[2,1,3]{2,0,1:T(2,128)}, u32[]{:S(2)}, u32[]{:S(2)}) collective-permute-start(f32[2,1,3]{2,0,1:T(2,128)} %slice.186), channel_id=1, source_target_pairs={{0,8},{8,16},{16,24},{24,32},{32,40},{40,48},{48,56},{1,9},{9,17},... | collective-permute-start | bytes 80 | tf_op jit(solution)/shard_map/ppermute | solution.py:31
  74.0 4.6 %collective-permute-start.2 = (f32[2,512,64]{2,1,0:T(8,128)}, f32[2,512,64]{2,1,0:T(8,128)S(1)}, u32[]{:S(2)}, u32[]{:S(2)}) collective-permute-start(f32[2,512,64]{2,1,0:T(8,128)} %get-tuple-element.366), channel_id=1, source_target_pairs={{0,1},{1,2},{2,3},{3,4},{4,5},{5,6},{6,7},{8,9},{9,10},{10,11},{11... | collective-permute-start | bytes 786440 | tf_op jit(solution)/shard_map/ppermute | solution.py:22
  78.8 8.2 %collective-permute-done.3 = f32[2,512,64]{2,1,0:T(8,128)S(1)} collective-permute-done((f32[2,512,64]{2,1,0:T(8,128)}, f32[2,512,64]{2,1,0:T(8,128)S(1)}, u32[]{:S(2)}, u32[]{:S(2)}) %collective-permute-start.3) | collective-permute-done | bytes 262176 | tf_op jit(solution)/shard_map/ppermute | solution.py:23
  87.0 2.9 %collective-permute-start.8 = (f32[2,3,1]{2,0,1:T(2,128)S(1)}, f32[2,3,1]{2,0,1:T(2,128)S(1)}, u32[]{:S(2)}, u32[]{:S(2)}) collective-permute-start(f32[2,3,1]{2,0,1:T(2,128)S(1)} %slice.183), channel_id=1, source_target_pairs={{0,1},{1,2},{2,3},{3,4},{4,5},{5,6},{6,7},{8,9},{9,10},{10,11},{11... | collective-permute-start | bytes 80 | tf_op jit(solution)/shard_map/ppermute | solution.py:31
  95.9 2.9 %collective-permute-start.9 = (f32[2,2,5,1]{3,2,1,0:T(8,128)S(1)}, f32[2,2,5,1]{3,2,1,0:T(8,128)S(1)}, u32[]{:S(2)}, u32[]{:S(2)}) collective-permute-start(f32[2,2,5,1]{3,2,1,0:T(8,128)S(1)} %get-tuple-element.375), channel_id=1, source_target_pairs={{0,1},{1,2},{2,3},{3,4},{4,5},{5,6},{6,7},{8,9},{9,10},{10,11},{11... | collective-permute-start | bytes 248 | tf_op jit(solution)/shard_map/ppermute | solution.py:22
  100.2 6.4 %collective-permute-done.4 = f32[1,512,512]{2,1,0:T(8,128)S(1)} collective-permute-done((f32[1,512,512]{2,1,0:T(8,128)S(1)}, f32[1,512,512]{2,1,0:T(8,128)S(1)}, u32[]{:S(2)}, u32[]{:S(2)}) %collective-permute-start.4) | collective-permute-done | bytes 1048608 | tf_op jit(solution)/shard_map/ppermute | solution.py:31
  108.1 62.9 %while.31 = (s32[]{:T(128)}, f32[2,512,512]{2,1,0:T(8,128)}, s32[18,3]{0,1:T(4,128)S(1)}, f32[18,128,128]{2,1,0:T(8,128)S(1)}, s32[]{:T(128)}) while((s32[]{:T(128)}, f32[2,512,512]{2,1,0:T(8,128)}, s32[18,3]{0,1:T(4,128)S(1)}, f32[18,128,128]{2,1,0:T(8,128)S(1)}, s32[]{:T(128)}) %tuple.119), condition=%wide.while_cond, body=%wide.while_body.sunk | while | flops 2 | bytes 131209 | solution.py:137
  108.8 2.8 dynamic-slice_dynamic-update-slice_fusion.2
  112.3 2.8 dynamic-slice_dynamic-update-slice_fusion.2
  115.7 2.8 dynamic-slice_dynamic-update-slice_fusion.2
  119.2 2.8 dynamic-slice_dynamic-update-slice_fusion.2
  122.7 2.8 dynamic-slice_dynamic-update-slice_fusion.2
  126.2 2.8 dynamic-slice_dynamic-update-slice_fusion.2
  129.7 2.8 dynamic-slice_dynamic-update-slice_fusion.2
  133.2 2.8 dynamic-slice_dynamic-update-slice_fusion.2
  136.7 2.8 dynamic-slice_dynamic-update-slice_fusion.2
  140.2 2.8 dynamic-slice_dynamic-update-slice_fusion.2
  143.7 2.8 dynamic-slice_dynamic-update-slice_fusion.2
  147.2 2.8 dynamic-slice_dynamic-update-slice_fusion.2
  150.7 2.8 dynamic-slice_dynamic-update-slice_fusion.2
  161.2 2.8 dynamic-slice_dynamic-update-slice_fusion.2
  171.1 38.5 %while.32 = (s32[]{:T(128)}, f32[2,9]{1,0:T(2,128)S(1)}, f32[2,9]{1,0:T(2,128)S(1)}, f32[2,9,128,128]{3,2,1,0:T(8,128)S(1)}, f32[2,9,128,128]{3,2,1,0:T(8,128)S(1)}, /*index=5*/s32[]{:T(128)}, s32[]{:T(128)}) while((s32[]{:T(128)}, f32[2,9]{1,0:T(2,128)S(1)}, f32[2,9]{1,0:T(2,128)S(1)}, ...), condition=%wide.region_7.8_spmd.clone.clone, body=%wide.region_0.7_spmd.clone.clone.sunk | while | flops 4085270272 | bytes 29495104 | solution.py:147
  210.5 12.8 %all-gather = f32[16,3,3]{2,1,0:T(4,128)S(1)} all-gather(f32[2,3,3]{2,1,0:T(4,128)S(1)} %get-tuple-element.351), channel_id=2, replica_groups=mesh['sec'=8,'row'=8,'col'=8] {'sec'}, dimensions={0}, use_global_device_ids=true | all-gather | bytes 648 | tf_op jit(solution)/shard_map/all_gather | solution.py:36
  228.2 12.9 %collective-permute-done.12 = f32[2,2,1,3]{3,2,1,0:T(1,128)S(1)} collective-permute-done((f32[2,2,1,3]{3,2,1,0:T(1,128)S(1)}, f32[2,2,1,3]{3,2,1,0:T(1,128)S(1)}, u32[]{:S(2)}, u32[]{:S(2)}) %collective-permute-start.12) | collective-permute-done | bytes 80 | tf_op jit(solution)/shard_map/ppermute | solution.py:23
  241.2 2.9 %collective-permute-start.14 = (f32[2,2,5,1]{3,2,1,0:T(8,128)S(1)}, f32[2,2,5,1]{3,2,1,0:T(8,128)S(1)}, u32[]{:S(2)}, u32[]{:S(2)}) collective-permute-start(f32[2,2,5,1]{3,2,1,0:T(8,128)S(1)} %get-tuple-element.373), channel_id=1, source_target_pairs={{0,1},{1,2},{2,3},{3,4},{4,5},{5,6},{6,7},{8,9},{9,10},{10,11},{11... | collective-permute-start | bytes 248 | tf_op jit(solution)/shard_map/ppermute | solution.py:22
  245.5 4.8 %collective-permute-done.13 = f32[2,2,5,1]{3,2,1,0:T(8,128)S(1)} collective-permute-done((f32[2,2,5,1]{3,2,1,0:T(8,128)S(1)}, f32[2,2,5,1]{3,2,1,0:T(8,128)S(1)}, u32[]{:S(2)}, u32[]{:S(2)}) %collective-permute-start.13) | collective-permute-done | bytes 112 | tf_op jit(solution)/shard_map/ppermute | solution.py:23
  250.5 11.9 %collective-permute-start.15 = (f32[2,2,1,3]{3,2,1,0:T(1,128)S(1)}, f32[2,2,1,3]{3,2,1,0:T(1,128)S(1)}, u32[]{:S(2)}, u32[]{:S(2)}) collective-permute-start(f32[2,2,1,3]{3,2,1,0:T(1,128)S(1)} %get-tuple-element.377), channel_id=1, source_target_pairs={{0,8},{8,16},{16,24},{24,32},{32,40},{40,48},{48,56},{1,9},{9,17},... | collective-permute-start | bytes 152 | tf_op jit(solution)/shard_map/ppermute | solution.py:22
  263.8 12.9 %collective-permute-done.16 = f32[2,2,1,3]{3,2,1,0:T(1,128)S(1)} collective-permute-done((f32[2,2,1,3]{3,2,1,0:T(1,128)S(1)}, f32[2,2,1,3]{3,2,1,0:T(1,128)S(1)}, u32[]{:S(2)}, u32[]{:S(2)}) %collective-permute-start.16) | collective-permute-done | bytes 80 | tf_op jit(solution)/shard_map/ppermute | solution.py:23
  276.7 3.9 %collective-permute-start.18 = (f32[2,2,5,1]{3,2,1,0:T(8,128)S(1)}, f32[2,2,5,1]{3,2,1,0:T(8,128)S(1)}, u32[]{:S(2)}, u32[]{:S(2)}) collective-permute-start(f32[2,2,5,1]{3,2,1,0:T(8,128)S(1)} %get-tuple-element.371), channel_id=1, source_target_pairs={{0,1},{1,2},{2,3},{3,4},{4,5},{5,6},{6,7},{8,9},{9,10},{10,11},{11... | collective-permute-start | bytes 248 | tf_op jit(solution)/shard_map/ppermute | solution.py:22
  282.1 4.2 %collective-permute-done.17 = f32[2,2,5,1]{3,2,1,0:T(8,128)S(1)} collective-permute-done((f32[2,2,5,1]{3,2,1,0:T(8,128)S(1)}, f32[2,2,5,1]{3,2,1,0:T(8,128)S(1)}, u32[]{:S(2)}, u32[]{:S(2)}) %collective-permute-start.17) | collective-permute-done | bytes 112 | tf_op jit(solution)/shard_map/ppermute | solution.py:23
  (225 shorter events, 109.9 us)
Async XLA Ops:
  2.4 53.4 %copy-start.2 = (f32[2,2,3,3]{3,1,2,0:T(2,128)S(1)}, f32[2,2,3,3]{3,1,2,0:T(2,128)}, u32[]{:S(2)}) copy-start(f32[2,2,3,3]{3,1,2,0:T(2,128)} %param.11) | copy-start | bytes 436
  2.4 65.9 %collective-permute-start = (f32[2,64,384]{2,1,0:T(8,128)}, f32[2,64,384]{2,1,0:T(8,128)}, u32[]{:S(2)}, u32[]{:S(2)}) collective-permute-start(f32[2,64,384]{2,1,0:T(8,128)} %get-tuple-element.369), channel_id=1, source_target_pairs={{0,8},{8,16},{16,24},{24,32},{32,40},{40,48},{48,56},{1,9},{9,17},... | collective-permute-start | bytes 589832 | tf_op jit(solution)/shard_map/ppermute | solution.py:22
  18.9 50.4 %collective-permute-start.1 = (f32[2,64,384]{2,1,0:T(8,128)}, f32[2,64,384]{2,1,0:T(8,128)}, u32[]{:S(2)}, u32[]{:S(2)}) collective-permute-start(f32[2,64,384]{2,1,0:T(8,128)} %get-tuple-element.368), channel_id=1, source_target_pairs={{8,0},{16,8},{24,16},{32,24},{40,32},{48,40},{56,48},{9,1},{17,9},... | collective-permute-start | bytes 589832 | tf_op jit(solution)/shard_map/ppermute | solution.py:23
  21.5 73.7 %collective-permute-start.5 = (f32[2,2,1,3]{3,2,1,0:T(1,128)}, f32[2,2,1,3]{3,2,1,0:T(1,128)}, u32[]{:S(2)}, u32[]{:S(2)}) collective-permute-start(f32[2,2,1,3]{3,2,1,0:T(1,128)} %bitcast.4), channel_id=1, source_target_pairs={{0,8},{8,16},{16,24},{24,32},{32,40},{40,48},{48,56},{1,9},{9,17},... | collective-permute-start | bytes 152 | tf_op jit(solution)/shard_map/ppermute | solution.py:22
  35.3 59.9 %collective-permute-start.6 = (f32[2,2,1,3]{3,2,1,0:T(1,128)}, f32[2,2,1,3]{3,2,1,0:T(1,128)}, u32[]{:S(2)}, u32[]{:S(2)}) collective-permute-start(f32[2,2,1,3]{3,2,1,0:T(1,128)} %bitcast.5), channel_id=1, source_target_pairs={{8,0},{16,8},{24,16},{32,24},{40,32},{48,40},{56,48},{9,1},{17,9},... | collective-permute-start | bytes 152 | tf_op jit(solution)/shard_map/ppermute | solution.py:23
  36.6 19.8 %copy-start.7 = (pred[3]{0:T(512)(128)(4,1)}, pred[3]{0:T(512)(128)(4,1)S(1)}, u32[]{:S(2)}) copy-start(pred[3]{0:T(512)(128)(4,1)S(1)} %get-tuple-element.392) | copy-start | bytes 13
  36.6 19.8 %copy-start.9 = (pred[3]{0:T(512)(128)(4,1)}, pred[3]{0:T(512)(128)(4,1)S(1)}, u32[]{:S(2)}) copy-start(pred[3]{0:T(512)(128)(4,1)S(1)} %get-tuple-element.393) | copy-start | bytes 13
  37.9 56.5 %collective-permute-start.10 = (f32[2,1,3]{2,0,1:T(2,128)}, f32[2,1,3]{2,0,1:T(2,128)}, u32[]{:S(2)}, u32[]{:S(2)}) collective-permute-start(f32[2,1,3]{2,0,1:T(2,128)} %slice.186), channel_id=1, source_target_pairs={{0,8},{8,16},{16,24},{24,32},{32,40},{40,48},{48,56},{1,9},{9,17},... | collective-permute-start | bytes 80 | tf_op jit(solution)/shard_map/ppermute | solution.py:31
  56.4 12.8 %copy-start = (f32[2,384,384]{2,1,0:T(8,128)S(1)}, f32[2,384,384]{2,1,0:T(8,128)}, u32[]{:S(2)}) copy-start(f32[2,384,384]{2,1,0:T(8,128)} %param.9) | copy-start | bytes 3538948
  69.3 9.2 %copy-start.11 = (s32[2,9,1]{1,0,2:T(2,128)S(1)}, s32[2,9,1]{1,0,2:T(2,128)}, u32[]{:S(2)}) copy-start(s32[2,9,1]{1,0,2:T(2,128)} %squeeze.33) | copy-start | bytes 220
  69.3 9.2 %copy-start.12 = (s32[2,9,1]{1,0,2:T(2,128)S(1)}, s32[2,9,1]{1,0,2:T(2,128)}, u32[]{:S(2)}) copy-start(s32[2,9,1]{1,0,2:T(2,128)} %squeeze.32) | copy-start | bytes 220
  69.4 9.2 %copy-start.14 = (s32[9]{0:T(128)S(1)}, s32[9]{0:T(128)}, u32[]{:S(2)}) copy-start(s32[9]{0:T(128)} %add.301) | copy-start | bytes 112
  69.4 9.2 %copy-start.15 = (s32[9]{0:T(128)S(1)}, s32[9]{0:T(128)}, u32[]{:S(2)}) copy-start(s32[9]{0:T(128)} %add.296) | copy-start | bytes 112
  72.7 14.4 %collective-permute-start.3 = (f32[2,512,64]{2,1,0:T(8,128)}, f32[2,512,64]{2,1,0:T(8,128)S(1)}, u32[]{:S(2)}, u32[]{:S(2)}) collective-permute-start(f32[2,512,64]{2,1,0:T(8,128)} %get-tuple-element.367), channel_id=1, source_target_pairs={{1,0},{2,1},{3,2},{4,3},{5,4},{6,5},{7,6},{9,8},{10,9},{11,10},{12... | collective-permute-start | bytes 786440 | tf_op jit(solution)/shard_map/ppermute | solution.py:23
  74.0 16.0 %collective-permute-start.2 = (f32[2,512,64]{2,1,0:T(8,128)}, f32[2,512,64]{2,1,0:T(8,128)S(1)}, u32[]{:S(2)}, u32[]{:S(2)}) collective-permute-start(f32[2,512,64]{2,1,0:T(8,128)} %get-tuple-element.366), channel_id=1, source_target_pairs={{0,1},{1,2},{2,3},{3,4},{4,5},{5,6},{6,7},{8,9},{9,10},{10,11},{11... | collective-permute-start | bytes 786440 | tf_op jit(solution)/shard_map/ppermute | solution.py:22
  87.0 8.1 %collective-permute-start.8 = (f32[2,3,1]{2,0,1:T(2,128)S(1)}, f32[2,3,1]{2,0,1:T(2,128)S(1)}, u32[]{:S(2)}, u32[]{:S(2)}) collective-permute-start(f32[2,3,1]{2,0,1:T(2,128)S(1)} %slice.183), channel_id=1, source_target_pairs={{0,1},{1,2},{2,3},{3,4},{4,5},{5,6},{6,7},{8,9},{9,10},{10,11},{11... | collective-permute-start | bytes 80 | tf_op jit(solution)/shard_map/ppermute | solution.py:31
  92.2 2.3 copy-start.6
  92.3 14.2 %collective-permute-start.4 = (f32[1,512,512]{2,1,0:T(8,128)S(1)}, f32[1,512,512]{2,1,0:T(8,128)S(1)}, u32[]{:S(2)}, u32[]{:S(2)}) collective-permute-start(f32[1,512,512]{2,1,0:T(8,128)S(1)} %get-tuple-element.365), channel_id=1, source_target_pairs={{64,0},{128,64},{192,128},{256,192},{320,256},{384,320},{448,384},... | collective-permute-start | bytes 3145736 | tf_op jit(solution)/shard_map/ppermute | solution.py:31
  95.9 127.7 %collective-permute-start.9 = (f32[2,2,5,1]{3,2,1,0:T(8,128)S(1)}, f32[2,2,5,1]{3,2,1,0:T(8,128)S(1)}, u32[]{:S(2)}, u32[]{:S(2)}) collective-permute-start(f32[2,2,5,1]{3,2,1,0:T(8,128)S(1)} %get-tuple-element.375), channel_id=1, source_target_pairs={{0,1},{1,2},{2,3},{3,4},{4,5},{5,6},{6,7},{8,9},{9,10},{10,11},{11... | collective-permute-start | bytes 248 | tf_op jit(solution)/shard_map/ppermute | solution.py:22
  98.9 124.7 %collective-permute-start.7 = (f32[2,2,5,1]{3,2,1,0:T(8,128)S(1)}, f32[2,2,5,1]{3,2,1,0:T(8,128)S(1)}, u32[]{:S(2)}, u32[]{:S(2)}) collective-permute-start(f32[2,2,5,1]{3,2,1,0:T(8,128)S(1)} %get-tuple-element.374), channel_id=1, source_target_pairs={{1,0},{2,1},{3,2},{4,3},{5,4},{6,5},{7,6},{9,8},{10,9},{11,10},{12... | collective-permute-start | bytes 248 | tf_op jit(solution)/shard_map/ppermute | solution.py:23
  106.6 64.5 %copy-start.17 = (f32[2,9]{1,0:T(2,128)S(1)}, f32[2,9]{1,0:T(2,128)}, u32[]{:S(2)}) copy-start(f32[2,9]{1,0:T(2,128)} %custom-call.3) | copy-start | bytes 220
  106.6 64.5 %copy-start.18 = (f32[2,9]{1,0:T(2,128)S(1)}, f32[2,9]{1,0:T(2,128)}, u32[]{:S(2)}) copy-start(f32[2,9]{1,0:T(2,128)} %custom-call.4) | copy-start | bytes 220
  171.1 38.7 %copy-start.4 = (s32[2,2,3,3]{3,1,2,0:T(2,128)S(1)}, s32[2,2,3,3]{3,1,2,0:T(2,128)}, u32[]{:S(2)}) copy-start(s32[2,2,3,3]{3,1,2,0:T(2,128)} %param.10) | copy-start | bytes 436
  171.1 52.5 %copy-start.3 = (f32[2,2,3,3]{3,1,2,0:T(2,128)S(1)}, f32[2,2,3,3]{3,1,2,0:T(2,128)}, u32[]{:S(2)}) copy-start(f32[2,2,3,3]{3,1,2,0:T(2,128)} %param.11) | copy-start | bytes 436
  224.5 3.7 %collective-permute-start.11 = (f32[2,2,1,3]{3,2,1,0:T(1,128)S(1)}, f32[2,2,1,3]{3,2,1,0:T(1,128)S(1)}, u32[]{:S(2)}, u32[]{:S(2)}) collective-permute-start(f32[2,2,1,3]{3,2,1,0:T(1,128)S(1)} %get-tuple-element.379), channel_id=1, source_target_pairs={{0,8},{8,16},{16,24},{24,32},{32,40},{40,48},{48,56},{1,9},{9,17},... | collective-permute-start | bytes 152 | tf_op jit(solution)/shard_map/ppermute | solution.py:22
  226.9 14.2 %collective-permute-start.12 = (f32[2,2,1,3]{3,2,1,0:T(1,128)S(1)}, f32[2,2,1,3]{3,2,1,0:T(1,128)S(1)}, u32[]{:S(2)}, u32[]{:S(2)}) collective-permute-start(f32[2,2,1,3]{3,2,1,0:T(1,128)S(1)} %get-tuple-element.378), channel_id=1, source_target_pairs={{8,0},{16,8},{24,16},{32,24},{40,32},{48,40},{56,48},{9,1},{17,9},... | collective-permute-start | bytes 152 | tf_op jit(solution)/shard_map/ppermute | solution.py:23
  241.2 4.3 %collective-permute-start.14 = (f32[2,2,5,1]{3,2,1,0:T(8,128)S(1)}, f32[2,2,5,1]{3,2,1,0:T(8,128)S(1)}, u32[]{:S(2)}, u32[]{:S(2)}) collective-permute-start(f32[2,2,5,1]{3,2,1,0:T(8,128)S(1)} %get-tuple-element.373), channel_id=1, source_target_pairs={{0,1},{1,2},{2,3},{3,4},{4,5},{5,6},{6,7},{8,9},{9,10},{10,11},{11... | collective-permute-start | bytes 248 | tf_op jit(solution)/shard_map/ppermute | solution.py:22
  244.1 6.3 %collective-permute-start.13 = (f32[2,2,5,1]{3,2,1,0:T(8,128)S(1)}, f32[2,2,5,1]{3,2,1,0:T(8,128)S(1)}, u32[]{:S(2)}, u32[]{:S(2)}) collective-permute-start(f32[2,2,5,1]{3,2,1,0:T(8,128)S(1)} %get-tuple-element.372), channel_id=1, source_target_pairs={{1,0},{2,1},{3,2},{4,3},{5,4},{6,5},{7,6},{9,8},{10,9},{11,10},{12... | collective-permute-start | bytes 248 | tf_op jit(solution)/shard_map/ppermute | solution.py:23
  250.5 13.2 %collective-permute-start.15 = (f32[2,2,1,3]{3,2,1,0:T(1,128)S(1)}, f32[2,2,1,3]{3,2,1,0:T(1,128)S(1)}, u32[]{:S(2)}, u32[]{:S(2)}) collective-permute-start(f32[2,2,1,3]{3,2,1,0:T(1,128)S(1)} %get-tuple-element.377), channel_id=1, source_target_pairs={{0,8},{8,16},{16,24},{24,32},{32,40},{40,48},{48,56},{1,9},{9,17},... | collective-permute-start | bytes 152 | tf_op jit(solution)/shard_map/ppermute | solution.py:22
  262.4 14.2 %collective-permute-start.16 = (f32[2,2,1,3]{3,2,1,0:T(1,128)S(1)}, f32[2,2,1,3]{3,2,1,0:T(1,128)S(1)}, u32[]{:S(2)}, u32[]{:S(2)}) collective-permute-start(f32[2,2,1,3]{3,2,1,0:T(1,128)S(1)} %get-tuple-element.376), channel_id=1, source_target_pairs={{8,0},{16,8},{24,16},{32,24},{40,32},{48,40},{56,48},{9,1},{17,9},... | collective-permute-start | bytes 152 | tf_op jit(solution)/shard_map/ppermute | solution.py:23
  276.7 5.4 %collective-permute-start.18 = (f32[2,2,5,1]{3,2,1,0:T(8,128)S(1)}, f32[2,2,5,1]{3,2,1,0:T(8,128)S(1)}, u32[]{:S(2)}, u32[]{:S(2)}) collective-permute-start(f32[2,2,5,1]{3,2,1,0:T(8,128)S(1)} %get-tuple-element.371), channel_id=1, source_target_pairs={{0,1},{1,2},{2,3},{3,4},{4,5},{5,6},{6,7},{8,9},{9,10},{10,11},{11... | collective-permute-start | bytes 248 | tf_op jit(solution)/shard_map/ppermute | solution.py:22
  280.7 5.6 %collective-permute-start.17 = (f32[2,2,5,1]{3,2,1,0:T(8,128)S(1)}, f32[2,2,5,1]{3,2,1,0:T(8,128)S(1)}, u32[]{:S(2)}, u32[]{:S(2)}) collective-permute-start(f32[2,2,5,1]{3,2,1,0:T(8,128)S(1)} %get-tuple-element.370), channel_id=1, source_target_pairs={{1,0},{2,1},{3,2},{4,3},{5,4},{6,5},{7,6},{9,8},{10,9},{11,10},{12... | collective-permute-start | bytes 248 | tf_op jit(solution)/shard_map/ppermute | solution.py:23
  (6 other events, 10.5 us)
where the time goes:
time: 291 us; the launch traced here: 287 us
  local copies, waits for them, and re-layouts  89.2 us (31%)
  starting transfers between devices  87.9 us (30%)
  waiting for transfers between devices  49.8 us (17%)
  matrix products  36.8 us (13%)
  blocking collectives  12.8 us (4%)
  other arithmetic  8.4 us (3%)
    gather x54, local copies, waits for them, and re-layouts  62.6 us
    ppermute x8, starting transfers between devices, extended(): before = lax.ppermute(last, axis, up)  59 us
    ppermute x8, waiting for transfers between devices, extended(): after = lax.ppermute(first, axis, down)  43.1 us
    dot_general x20, matrix products, left_mul(): jnp.einsum('jy,nyk->njk', table, blocks, precision=lax.Precision.HIGHEST)  19.2 us
    ppermute x3, starting transfers between devices, shifted(): return lax.ppermute(block, axis, route)  18.6 us
    dot_general x16, matrix products, right_mul(): jnp.einsum('nyx,xk->nyk', blocks, table, precision=lax.Precision.HIGHEST)  17.6 us
    all_gather x1, blocking collectives, prefix(): everything = lax.all_gather(shard, axis)  12.8 us
    ppermute x8, starting transfers between devices, extended(): after = lax.ppermute(first, axis, down)  10.3 us
  transfers between devices with their start and end apart: 19, of which 8 were waited for; matrix products, arithmetic and copies ran while one was open for 45% of the time, Pallas kernels for 0%

commit v1 on v0

v1 whole, which is shorter than its diff:
```python
import functools

import jax
import jax.numpy as jnp
import ml_dtypes
import numpy as np
from jax import lax
from jax.experimental import pallas as pl
from jax.experimental.pallas import tpu as pltpu
from jax.sharding import PartitionSpec as P

MESH = pl.DeviceIdType.MESH
N = 128
HALF = 64
SIDE = 3
TILE = SIDE * N
BLOCKS = 2 * TILE // N
SHARPNESS = 80.0
ANCHOR = 0.2
ITERS = 3
BF = jnp.bfloat16
F32 = jnp.float32


def split3(a):
    high = a.astype(ml_dtypes.bfloat16)
    rest = a - high.astype(np.float64)
    mid = rest.astype(ml_dtypes.bfloat16)
    low = (rest - mid.astype(np.float64)).astype(ml_dtypes.bfloat16)
    return high, mid, low


def tables():
    x = np.arange(N)
    forward = np.zeros((N, N))
    for f in range(HALF):
        forward[f] = np.cos(2 * np.pi * ((f * x) % N) / N)
    forward[HALF] = 1 - 2 * (x % 2)
    for f in range(1, HALF):
        forward[HALF + f] = np.sin(2 * np.pi * ((f * x) % N) / N)
    scale = np.full(N, 2.0 / N)
    scale[0] = scale[HALF] = 1.0 / N
    inverse = (forward * scale[:, None]).T

    def right(a):
        h, m, l = split3(a)
        return np.block([[h, m], [h, m]]), np.concatenate([h, l], 0)

    def left(a):
        h, m, l = split3(a)
        return np.concatenate([h, m], 1), np.concatenate([h, l], 1)

    return (
        *right(forward.T),
        *left(forward),
        *right(inverse.T),
        *left(inverse * (SHARPNESS / (N * N))),
    )


def parts(x):
    high = x.astype(BF)
    rest = x - high.astype(F32)
    mid = rest.astype(BF)
    low = (rest - mid.astype(F32)).astype(BF)
    return high, mid, low


def dot(a, b):
    return jnp.dot(a, b, preferred_element_type=F32)


def right_mul(x, wa, wb):
    high, mid, low = parts(x)
    a = dot(jnp.concatenate([high, mid], 1), wa)
    return a[:, :N] + a[:, N:] + dot(jnp.concatenate([low, high], 1), wb)


def left_mul(wa, wb, x):
    high, mid, low = parts(x)
    row = jnp.concatenate([high, mid], 1)
    a = dot(wa, jnp.concatenate([row, row], 0))
    return a[:, :N] + a[:, N:] + dot(wb, jnp.concatenate([low, high], 0))


def forward(x, t):
    x = x - jnp.sum(x, keepdims=True) * (1.0 / (N * N))
    return left_mul(t[2][...], t[3][...], right_mul(x, t[0][...], t[1][...]))


def inverse(x, t):
    return left_mul(t[6][...], t[7][...], right_mul(x, t[4][...], t[5][...]))


def iota(shape, dim):
    return lax.broadcasted_iota(jnp.int32, shape, dim)


def swap(x):
    return pltpu.roll(x, HALF, 1)


def cross(mine, theirs):
    lane = iota((N, N), 1)
    single = (lane & (HALF - 1)) == 0
    turned = swap(theirs)
    first = jnp.where(single | (lane < HALF), theirs, -turned)
    second = jnp.where(single, 0.0, jnp.where(lane < HALF, turned, theirs))
    other = swap(mine)
    even, odd = slice(0, HALF), slice(HALF, N)

    def pair(a, b):
        return mine[a] * first[b] + other[a] * second[b]

    lone = iota((HALF, N), 0) == 0
    both = pair(odd, odd)
    top = pair(even, even) + jnp.where(lone, 0.0, both)
    low = jnp.where(lone, both, pair(even, odd) - pair(odd, even))
    return jnp.concatenate([top, low], 0)


def peak(scores, dy, dx):
    rows = (((iota((N, N), 0) - dy + HALF) & (N - 1)) - HALF).astype(F32)
    cols = (((iota((1, N), 1) - dx + HALF) & (N - 1)) - HALF).astype(F32)
    weights = jnp.exp(scores - jnp.max(scores, keepdims=True))
    by_col = jnp.sum(weights, axis=0, keepdims=True)
    total = jnp.sum(by_col, keepdims=True)
    along_rows = jnp.sum(jnp.sum(weights * rows, axis=0, keepdims=True), keepdims=True)
    along_cols = jnp.sum(by_col * cols, keepdims=True)
    return along_rows / total, along_cols / total


def kernel(sizes, images, off, warp, stiff, valid, *rest):
    t = rest[:8]
    disp_ref, warped_ref = rest[8:10]
    (own, ext, spec, packed, landed, small, ptile, pslots, ttile, tslots, dtile, dslots, strips) = rest[10:23]
    lsem, ts, tr, rs, rr, cs, cr, ks, kr, ps, pr, ds, dr, ns, nr = rest[23:]
    ns_, nr_, nc_ = sizes
    s, r, c = lax.axis_index("sec"), lax.axis_index("row"), lax.axis_index("col")

    def inside(a, b, e):
        ok = None
        for at, by, n in ((s, a, ns_), (r, b, nr_), (c, e, nc_)):
            if by:
                here = (at + by >= 0) & (at + by < n)
                ok = here if ok is None else ok & here
        return ok

    def there(a, b, e):
        return (s + a, r + b, c + e)

    locals_ = [
        pltpu.make_async_copy(images.at[0], own, lsem.at[0]),
        pltpu.make_async_copy(images.at[1], ext.at[0, HALF : HALF + TILE, N : N + TILE], lsem.at[1]),
    ]
    for copy in locals_:
        copy.start()

    near = [(a, b) for a in (-1, 0, 1) for b in (-1, 0, 1) if (a, b) != (0, 0)]
    sides = [(-1, 0), (1, 0), (0, -1), (0, 1)]
    goes = [(k, 0, 0) for k in range(1, ns_)] + [(-1, 0, 0)] + [(-1, b, e) for b, e in sides] + [(0, b, e) for b, e in near]
    barrier = pltpu.get_barrier_semaphore()
    expected = 0
    for a, b, e in goes:
        @pl.when(inside(-a, -b, -e))
        def _(a=a, b=b, e=e):
            pl.semaphore_signal(barrier, inc=1, device_id=there(-a, -b, -e), device_id_type=MESH)

        expected = expected + inside(a, b, e).astype(jnp.int32)

    @pl.when(r == 0)
    def _():
        for p in range(2):
            ext[p, 0:HALF, :] = jnp.zeros((HALF, TILE + 2 * N), F32)

    @pl.when(r == nr_ - 1)
    def _():
        for p in range(2):
            ext[p, HALF + TILE :, :] = jnp.zeros((HALF, TILE + 2 * N), F32)

    @pl.when(c == 0)
    def _():
        for p in range(2):
            ext[p, 0:HALF, 0:N] = jnp.zeros((HALF, N), F32)
            ext[p, HALF + TILE :, 0:N] = jnp.zeros((HALF, N), F32)
            landed[p, 0] = jnp.zeros((TILE // 2, N), F32)

    @pl.when(c == nc_ - 1)
    def _():
        for p in range(2):
            ext[p, 0:HALF, N + TILE :] = jnp.zeros((HALF, N), F32)
            ext[p, HALF + TILE :, N + TILE :] = jnp.zeros((HALF, N), F32)
            landed[p, 1] = jnp.zeros((TILE // 2, N), F32)

    @pl.when(s == ns_ - 1)
    def _():
        ext[1] = jnp.zeros((TILE + 2 * HALF, TILE + 2 * N), F32)
        landed[1] = jnp.zeros((2, TILE // 2, N), F32)

    blank = jnp.zeros((8, N), F32)
    for b, e in near:
        @pl.when(jnp.logical_not(inside(0, b, e)))
        def _(b=b, e=e):
            pslots[3 * (b + 1) + e + 1] = blank
            tslots[3 * (b + 1) + e + 1] = blank

    for k in range(ns_):
        @pl.when(s <= k)
        def _(k=k):
            dslots[k] = blank

    row8, lane8 = iota((8, N), 0), iota((8, N), 1)
    small[...] = jnp.zeros_like(small)
    for comp in range(2):
        for sec in range(2):
            small[2 * comp + sec, 0:SIDE, 0:SIDE] = warp[comp, sec]
            small[4 + 2 * comp + sec, 0:SIDE, 0:SIDE] = stiff[comp, sec]
    for sec in range(2):
        small[8 + sec, 0:SIDE, 0:SIDE] = ANCHOR * valid[sec].astype(F32)
    start = jnp.zeros((8, N), F32)
    held = jnp.zeros((8, N), F32)
    for g in range(4):
        sec = g % 2
        w = small[g]
        right = jnp.where((c == nc_ - 1) & (lane8 == SIDE - 1), 0.0, small[4 + sec])
        down = jnp.where((r == nr_ - 1) & (row8 == SIDE - 1), 0.0, small[6 + sec])
        start = start + (pltpu.roll(w, 16 * g, 1) if g else w)
        for q, quantity in enumerate((w, right, down, small[8 + sec])):
            by = 16 * g + SIDE * q
            held = held + (pltpu.roll(quantity, by, 1) if by else quantity)
    ptile[...] = held

    for copy in locals_:
        copy.wait()

    low_lane = iota((TILE // 2, N), 1) < HALF
    for im in range(2):
        for side in range(2):
            if im == 0:
                strip = own[:, 0:N] if side == 0 else own[:, TILE - N :]
            else:
                strip = ext[0, HALF : HALF + TILE, N : 2 * N] if side == 0 else ext[0, HALF : HALF + TILE, TILE : TILE + N]
            upper, lower = strip[: TILE // 2], strip[TILE // 2 :]
            packed[im, side] = jnp.where(low_lane, upper, swap(lower)) if side == 0 else jnp.where(low_lane, swap(upper), lower)

    def mine_spectra(p):
        def step(k, _):
            i, j = k // SIDE, k % SIDE
            at = pl.multiple_of(i * N, N)
            if p == 0:
                block = own[pl.ds(at, N), pl.ds(pl.multiple_of(j * N, N), N)]
            else:
                block = ext[0, pl.ds(pl.multiple_of(at + HALF, HALF), N), pl.ds(pl.multiple_of(j * N + N, N), N)]
            spec[9 * p + k] = forward(block, t)
            return 0

        lax.fori_loop(0, SIDE * SIDE, step, 0)

    mine_spectra(0)

    pl.semaphore_wait(barrier, expected)

    def remote(src, dst, send, recv, target):
        return pltpu.make_async_remote_copy(
            src_ref=src, dst_ref=dst, send_sem=send, recv_sem=recv, device_id=target, device_id_type=MESH
        )

    def col_rim(p, side):
        e = 2 * side - 1
        return remote(
            packed.at[1 - p, side], landed.at[p, 1 - side], cs.at[2 * p + side], cr.at[2 * p + 1 - side], there(-p, 0, e)
        )

    def row_rim(p, side):
        b = 2 * side - 1
        src = images.at[1 - p, TILE - HALF : TILE, :] if side else images.at[1 - p, 0:HALF, :]
        at = slice(0, HALF) if side else slice(HALF + TILE, 2 * HALF + TILE)
        return remote(src, ext.at[p, at, N : N + TILE], rs.at[2 * p + side], rr.at[2 * p + 1 - side], there(-p, b, 0))

    def corner(p, end, side):
        e = 2 * side - 1
        at = slice(HALF + TILE, 2 * HALF + TILE) if end else slice(0, HALF)
        src = slice(TILE, TILE + N) if side else slice(N, 2 * N)
        dst = slice(0, N) if side else slice(N + TILE, 2 * N + TILE)
        n = 4 * p + 2 * end
        return remote(ext.at[p, at, src], ext.at[p, at, dst], ks.at[n + side], kr.at[n + 1 - side], there(0, 0, e))

    def tile_copy():
        return remote(images.at[0], ext.at[1, HALF : HALF + TILE, N : N + TILE], ts.at[0], tr.at[0], there(-1, 0, 0))

    def frame_copy(src, slots, send, recv, b, e):
        n, m = 3 * (b + 1) + e + 1, 3 * (1 - b) + 1 - e
        return remote(src, slots.at[m], send.at[n], recv.at[m], there(0, b, e))

    for b, e in near:
        @pl.when(inside(0, b, e))
        def _(b=b, e=e):
            frame_copy(ptile, pslots, ps, pr, b, e).start()

    for p in (0, 1):
        for side in range(2):
            @pl.when(inside(-p, 0, 2 * side - 1))
            def _(p=p, side=side):
                col_rim(p, side).start()
    for p in (1, 0):
        for side in range(2):
            @pl.when(inside(-p, 2 * side - 1, 0))
            def _(p=p, side=side):
                row_rim(p, side).start()

    @pl.when(s > 0)
    def _():
        tile_copy().start()

    mine_spectra(1)

    def match_row(p, i):
        lane = iota((N, N), 1)
        row = iota((N, N), 0)
        low = lane < HALF
        found = dtile[...]
        top = HALF + i * N
        for j in range(SIDE):
            def at(rows, block):
                return ext[p, rows, block * N : block * N + N]

            def beside(rows, width):
                left, right = at(rows, j), at(rows, j + 2)
                return jnp.where(low[:width], right, left)

            centre = slice(top, top + N)
            above, below = slice(top - HALF, top), slice(top + N, top + N + HALF)
            dy, dx = off[0, p, i, j], off[1, p, i, j]
            in_rows = (row >= dy) & (row < dy + N)
            in_cols = (lane >= dx) & (lane < dx + N)
            main = jnp.where(in_cols, at(centre, j + 1), beside(centre, N))
            over = jnp.concatenate([at(below, j + 1), at(above, j + 1)], 0)
            over_side = jnp.concatenate([beside(below, HALF), beside(above, HALF)], 0)
            theirs = jnp.where(in_rows, main, jnp.where(in_cols, over, over_side))
            scores = inverse(cross(spec[9 * p + SIDE * i + j], forward(theirs, t)), t)
            peaks = peak(scores, dy, dx)
            for comp, (shift, by) in enumerate(zip(peaks, (dy, dx))):
                value = (by.astype(F32) + shift) * (1.0 / N)
                found = jnp.where((row8 == i) & (lane8 == 16 * (2 * comp + p) + j), value, found)
        dtile[...] = found

    dtile[...] = blank

    for p in (0, 1):
        for side in range(2):
            @pl.when(inside(p, 0, 1 - 2 * side))
            def _(p=p, side=side):
                col_rim(p, side).wait_recv()
        if p == 1:
            @pl.when(s < ns_ - 1)
            def _():
                tile_copy().wait_recv()
        for side in range(2):
            got = landed[p, side]
            column = slice(0, N) if side == 0 else slice(N + TILE, 2 * N + TILE)
            turned = swap(got)
            if side == 0:
                upper, lower = turned, got
            else:
                upper, lower = got, turned
            ext[p, HALF : HALF + TILE // 2, column] = upper
            ext[p, HALF + TILE // 2 : HALF + TILE, column] = lower
        match_row(p, 1)

    for p in (1, 0):
        for end in range(2):
            side = 1 - end
            @pl.when(inside(p, 1 - 2 * side, 0))
            def _(p=p, side=side):
                row_rim(p, side).wait_recv()

            for e in range(2):
                @pl.when(inside(p, 1 - 2 * side, 0) & inside(0, 0, 2 * e - 1))
                def _(p=p, end=end, e=e):
                    corner(p, end, e).start()
        for end in range(2):
            side = 1 - end
            for e in range(2):
                @pl.when(inside(p, 1 - 2 * side, 0) & inside(0, 0, 1 - 2 * e))
                def _(p=p, end=end, e=e):
                    corner(p, end, e).wait_recv()
            match_row(p, 2 * end)

    silent = (s == ns_ - 1) & ((lane8 & 16) != 0)
    found = jnp.where(silent, 0.0, dtile[...])
    dtile[...] = found

    def total_copy(k):
        return remote(dtile, dslots.at[s], ds.at[k], dr.at[s], (k, r, c))

    def total_arrival(k):
        return remote(dtile, dslots.at[k], ds.at[k], dr.at[k], (k, r, c))

    for k in range(ns_ - 1, 0, -1):
        @pl.when(k > s)
        def _(k=k):
            total_copy(k).start()
    for g in range(4):
        disp_ref[g // 2, g % 2] = (pltpu.roll(found, N - 16 * g, 1) if g else found)[0:SIDE, 0:SIDE]

    lane16 = iota((16, N), 1) & 15

    def frame(q):
        out = jnp.zeros((16, N), F32)
        for e in (-1, 0, 1):
            at = SIDE * (e + 1)
            by = (at - SIDE * q) % N
            strip = strips[e + 1]
            strip = pltpu.roll(strip, by, 1) if by else strip
            out = jnp.where((lane16 >= at) & (lane16 < at + SIDE), strip, out)
        return out

    def fill(centre, slots):
        for b in (-1, 0, 1):
            for e in (-1, 0, 1):
                at = SIDE * (b + 1)
                tile = centre[...] if (b, e) == (0, 0) else slots[3 * (b + 1) + e + 1]
                strips[e + 1, at : at + SIDE, :] = tile[0:SIDE]

    strips[...] = jnp.zeros_like(strips)
    for b, e in near:
        @pl.when(inside(0, b, e))
        def _(b=b, e=e):
            frame_copy(ptile, pslots, ps, pr, -b, -e).wait_recv()
    fill(ptile, pslots)
    v, right, down, anchor = (frame(q) for q in range(4))
    right_left = pltpu.roll(right, 1, 1)
    down_upper = pltpu.roll(down, 1, 0)

    for k in range(ns_ - 1):
        @pl.when(k < s)
        def _(k=k):
            total_arrival(k).wait_recv()
    lower = dslots[0]
    for k in range(1, ns_ - 1):
        lower = lower + dslots[k]
    second = (lane8 & 16) != 0
    below = lower + jnp.where(second, pltpu.roll(lower, 16, 1), pltpu.roll(lower, N - 16, 1))
    below = below + jnp.where(second, pltpu.roll(found, 16, 1), 0.0)
    ttile[...] = start - below
    for b, e in near:
        @pl.when(inside(0, b, e))
        def _(b=b, e=e):
            frame_copy(ttile, tslots, ns, nr, b, e).start()

    for p in (0, 1):
        for side in range(2):
            @pl.when(inside(-p, 0, 2 * side - 1))
            def _(p=p, side=side):
                col_rim(p, side).wait_send()

            @pl.when(inside(-p, 2 * side - 1, 0))
            def _(p=p, side=side):
                row_rim(p, side).wait_send()

            for e in range(2):
                @pl.when(inside(p, 2 * side - 1, 0) & inside(0, 0, 2 * e - 1))
                def _(p=p, side=side, e=e):
                    corner(p, side, e).wait_send()

    @pl.when(s > 0)
    def _():
        tile_copy().wait_send()

    for k in range(1, ns_):
        @pl.when(k > s)
        def _(k=k):
            total_copy(k).wait_send()
    for b, e in near:
        @pl.when(inside(0, b, e))
        def _(b=b, e=e):
            frame_copy(ptile, pslots, ps, pr, b, e).wait_send()
            frame_copy(ttile, tslots, ns, nr, b, e).wait_send()
            frame_copy(ttile, tslots, ns, nr, -b, -e).wait_recv()

    fill(ttile, tslots)
    target = frame(0)
    for _ in range(ITERS):
        v = (
            v
            + right * (pltpu.roll(v, N - 1, 1) - v)
            + right_left * (pltpu.roll(v, 1, 1) - v)
            + down * (pltpu.roll(v, 15, 0) - v)
            + down_upper * (pltpu.roll(v, 1, 0) - v)
            + anchor * (target - v)
        )
    v = pltpu.roll(v, 16 - SIDE, 0)
    for g in range(4):
        warped_ref[g // 2, g % 2] = pltpu.roll(v, (N - 16 * g - SIDE) % N, 1)[0:SIDE, 0:SIDE]


def per_device(sizes, images, offsets, warp, stiffness, valid):
    vmem = pl.BlockSpec(memory_space=pltpu.VMEM)
    dma = pltpu.SemaphoreType.DMA
    out = jax.ShapeDtypeStruct((2, 2, SIDE, SIDE), F32)
    n = sizes[0]
    return pl.pallas_call(
        functools.partial(kernel, sizes),
        name="align",
        out_shape=(out, out),
        in_specs=[pl.BlockSpec(memory_space=pl.ANY), pl.BlockSpec(memory_space=pltpu.SMEM)] + [vmem] * 11,
        out_specs=(vmem, vmem),
        scratch_shapes=[
            pltpu.VMEM((TILE, TILE), F32),
            pltpu.VMEM((2, TILE + 2 * HALF, TILE + 2 * N), F32),
            pltpu.VMEM((18, N, N), F32),
            pltpu.VMEM((2, 2, TILE // 2, N), F32),
            pltpu.VMEM((2, 2, TILE // 2, N), F32),
            pltpu.VMEM((10, 8, N), F32),
            pltpu.VMEM((8, N), F32),
            pltpu.VMEM((9, 8, N), F32),
            pltpu.VMEM((8, N), F32),
            pltpu.VMEM((9, 8, N), F32),
            pltpu.VMEM((8, N), F32),
            pltpu.VMEM((n, 8, N), F32),
            pltpu.VMEM((3, 16, N), F32),
            dma((2,)),
            dma((1,)),
            dma((1,)),
            dma((4,)),
            dma((4,)),
            dma((4,)),
            dma((4,)),
            dma((8,)),
            dma((8,)),
            dma((9,)),
            dma((9,)),
            dma((n,)),
            dma((n,)),
            dma((9,)),
            dma((9,)),
        ],
        compiler_params=pltpu.CompilerParams(
            collective_id=0, has_side_effects=True, vmem_limit_bytes=32 * 1024 * 1024
        ),
    )(images, offsets, warp, stiffness, valid, *(jnp.asarray(a) for a in tables()))


def solution(mesh):
    sizes = tuple(mesh.shape[a] for a in ("sec", "row", "col"))
    return jax.shard_map(
        functools.partial(per_device, sizes),
        mesh=mesh,
        in_specs=(
            P("sec", "row", "col"),
            P(None, "sec", "row", "col"),
            P(None, "sec", "row", "col"),
            P(None, "sec", "row", "col"),
            P("sec", "row", "col"),
        ),
        out_specs=(P(None, "sec", "row", "col"), P(None, "sec", "row", "col")),
        check_vma=False,
    )
```

time: 291 us -> 99.3 us (0.34)
  the two profiles are of different devices: /device:TPU:6 before, /device:TPU:30 now
where the time goes in v1:
time: 99.3 us; the launch traced here: 98.6 us
  Pallas kernels  85.9 us (87%)
  local copies, waits for them, and re-layouts  12.1 us (12%)
    pallas_call x1, Pallas kernels, per_device(): pl.pallas_call(functools.partial(kernel, sizes), name='align', out_shape=...  85.9 us
    unnamed x22, local copies, waits for them, and re-layouts  10.9 us

profile of v1, /device:TPU:30, one launch (start us, length us, event | category | flops | bytes accessed | tf_op | source)
XLA Modules:
  0.0 98.6 jit_solution(8631869833208604239)
XLA Ops:
  0.6 0.7 copy.18.valid
  1.3 0.7 copy.15.off
  2.0 0.7 copy.16.warp
  2.7 0.7 copy.17.stiff
  3.4 0.0 copy-start
  3.4 1.3 %copy-done = f32[2,384,384]{2,1,0:T(8,128)S(1)} copy-done((f32[2,384,384]{2,1,0:T(8,128)S(1)}, f32[2,384,384]{2,1,0:T(8,128)}, u32[]{:S(2)}) %copy-start) | copy-done | bytes 1179672
  4.7 0.0 copy-start.1
  4.7 0.9 copy-done.1
  5.6 0.0 copy-start.2
  5.6 0.9 copy-done.2
  6.5 0.0 copy-start.3
  6.5 0.8 copy-done.3
  7.3 0.0 copy-start.4
  7.3 0.8 copy-done.4
  8.2 0.0 copy-start.5
  8.2 0.8 copy-done.5
  9.0 0.0 copy-start.6
  9.0 0.8 copy-done.6
  9.8 0.0 copy-start.7
  9.8 0.8 copy-done.7
  10.7 0.0 copy-start.8
  10.7 0.8 copy-done.8
  11.5 85.9 %align.1 = (f32[2,2,3,3]{3,2,1,0:T(4,128)S(1)}, f32[2,2,3,3]{3,2,1,0:T(4,128)S(1)}) custom-call(f32[2,384,384]{2,1,0:T(8,128)S(1)} %copy-done, s32[2,2,3,3]{3,2,1,0:T(4,128)S(1)} %copy.15.off, f32[2,2,3,3]{3,2,1,0:T(4,128)S(1)} %copy.16.warp, f32[2,2,3,3]{3,2,1,0:T(4,128)S(1)} %copy.17.stiff, s32[2,3,3]{2,1,0:T(4,128)S(1)} %copy.18.valid, ...), custom_call_target="tpu_custom_call" | custom-call | tf_op jit(solution)/shard_map/align/pallas_call | solution.py:502
  97.5 0.6 copy.19
  98.1 0.6 copy.20
Async XLA Ops:
  3.4 1.3 %copy-start = (f32[2,384,384]{2,1,0:T(8,128)S(1)}, f32[2,384,384]{2,1,0:T(8,128)}, u32[]{:S(2)}) copy-start(f32[2,384,384]{2,1,0:T(8,128)} %images.1) | copy-start | bytes 3538948
  4.7 0.9 copy-start.1
  5.6 0.9 copy-start.2
  6.5 0.8 copy-start.3
  7.3 0.8 copy-start.4
  8.2 0.8 copy-start.5
  9.0 0.8 copy-start.6
  9.8 0.8 copy-start.7
  10.7 0.8 copy-start.8

commit v2 on v1

--- a/solution.py
+++ b/solution.py
@@ -46,16 +46,7 @@
         h, m, l = split3(a)
         return np.block([[h, m], [h, m]]), np.concatenate([h, l], 0)
 
-    def left(a):
-        h, m, l = split3(a)
-        return np.concatenate([h, m], 1), np.concatenate([h, l], 1)
-
-    return (
-        *right(forward.T),
-        *left(forward),
-        *right(inverse.T),
-        *left(inverse * (SHARPNESS / (N * N))),
-    )
+    return np.concatenate([*right(forward.T), *right(inverse.T * np.sqrt(SHARPNESS / (N * N)))], 1)
 
 
 def parts(x):
@@ -76,20 +67,16 @@
     return a[:, :N] + a[:, N:] + dot(jnp.concatenate([low, high], 1), wb)
 
 
-def left_mul(wa, wb, x):
-    high, mid, low = parts(x)
-    row = jnp.concatenate([high, mid], 1)
-    a = dot(wa, jnp.concatenate([row, row], 0))
-    return a[:, :N] + a[:, N:] + dot(wb, jnp.concatenate([low, high], 0))
+def turn(x):
+    return jnp.concatenate([x[k : k + N].T for k in range(0, x.shape[0], N)], 0)
 
 
 def forward(x, t):
-    x = x - jnp.sum(x, keepdims=True) * (1.0 / (N * N))
-    return left_mul(t[2][...], t[3][...], right_mul(x, t[0][...], t[1][...]))
+    return right_mul(turn(right_mul(x, t[:, 0 : 2 * N], t[:, 2 * N : 3 * N])), t[:, 0 : 2 * N], t[:, 2 * N : 3 * N])
 
 
 def inverse(x, t):
-    return left_mul(t[6][...], t[7][...], right_mul(x, t[4][...], t[5][...]))
+    return right_mul(turn(right_mul(x, t[:, 3 * N : 5 * N], t[:, 5 * N :])), t[:, 3 * N : 5 * N], t[:, 5 * N :])
 
 
 def iota(shape, dim):
@@ -115,26 +102,30 @@
     lone = iota((HALF, N), 0) == 0
     both = pair(odd, odd)
     top = pair(even, even) + jnp.where(lone, 0.0, both)
+    top = jnp.where(lone & (iota((HALF, N), 1) == 0), 0.0, top)
     low = jnp.where(lone, both, pair(even, odd) - pair(odd, even))
     return jnp.concatenate([top, low], 0)
 
 
-def peak(scores, dy, dx):
-    rows = (((iota((N, N), 0) - dy + HALF) & (N - 1)) - HALF).astype(F32)
-    cols = (((iota((1, N), 1) - dx + HALF) & (N - 1)) - HALF).astype(F32)
-    weights = jnp.exp(scores - jnp.max(scores, keepdims=True))
-    by_col = jnp.sum(weights, axis=0, keepdims=True)
-    total = jnp.sum(by_col, keepdims=True)
-    along_rows = jnp.sum(jnp.sum(weights * rows, axis=0, keepdims=True), keepdims=True)
-    along_cols = jnp.sum(by_col * cols, keepdims=True)
-    return along_rows / total, along_cols / total
-
-
-def kernel(sizes, images, off, warp, stiff, valid, *rest):
-    t = rest[:8]
-    disp_ref, warped_ref = rest[8:10]
-    (own, ext, spec, packed, landed, small, ptile, pslots, ttile, tslots, dtile, dslots, strips) = rest[10:23]
-    lsem, ts, tr, rs, rr, cs, cr, ks, kr, ps, pr, ds, dr, ns, nr = rest[23:]
+def peaks(scores, shifts):
+    count = len(shifts)
+    blocks = [scores[k * N : k * N + N] for k in range(count)]
+    highest = jnp.concatenate([jnp.max(x, axis=0, keepdims=True) for x in blocks], 0)
+    highest = jnp.max(highest, axis=1, keepdims=True)
+    sums = []
+    for k, (dy, dx) in enumerate(shifts):
+        rows = (((iota((N, N), 0) - dy + HALF) & (N - 1)) - HALF).astype(F32)
+        cols = (((iota((1, N), 1) - dx + HALF) & (N - 1)) - HALF).astype(F32)
+        weights = jnp.exp(blocks[k] - highest[k : k + 1])
+        by_col = jnp.sum(weights, axis=0, keepdims=True)
+        sums.append((by_col, jnp.sum(weights * rows, axis=0, keepdims=True), by_col * cols))
+    sums = [jnp.sum(jnp.concatenate([x[q] for x in sums], 0), axis=1, keepdims=True) for q in range(3)]
+    return sums[1] / sums[0], sums[2] / sums[0]
+
+
+def kernel(sizes, images, off, warp, stiff, valid, table, disp_ref, warped_ref, *rest):
+    (t, own, ext, spec, packed, landed, small, ptile, pslots, ttile, tslots, dtile, dslots, strips) = rest[:14]
+    lsem, ts, tr, rs, rr, cs, cr, ks, kr, ps, pr, ds, dr, ns, nr = rest[14:]
     ns_, nr_, nc_ = sizes
     s, r, c = lax.axis_index("sec"), lax.axis_index("row"), lax.axis_index("col")
 
@@ -152,6 +143,7 @@
     locals_ = [
         pltpu.make_async_copy(images.at[0], own, lsem.at[0]),
         pltpu.make_async_copy(images.at[1], ext.at[0, HALF : HALF + TILE, N : N + TILE], lsem.at[1]),
+        pltpu.make_async_copy(table, t, lsem.at[2]),
     ]
     for copy in locals_:
         copy.start()
@@ -213,10 +205,10 @@
     small[...] = jnp.zeros_like(small)
     for comp in range(2):
         for sec in range(2):
-            small[2 * comp + sec, 0:SIDE, 0:SIDE] = warp[comp, sec]
-            small[4 + 2 * comp + sec, 0:SIDE, 0:SIDE] = stiff[comp, sec]
+            small[2 * comp + sec, 0:SIDE, 0:SIDE] = warp[comp, :, sec]
+            small[4 + 2 * comp + sec, 0:SIDE, 0:SIDE] = stiff[comp, :, sec]
     for sec in range(2):
-        small[8 + sec, 0:SIDE, 0:SIDE] = ANCHOR * valid[sec].astype(F32)
+        small[8 + sec, 0:SIDE, 0:SIDE] = ANCHOR * valid[:, sec].astype(F32)
     start = jnp.zeros((8, N), F32)
     held = jnp.zeros((8, N), F32)
     for g in range(4):
@@ -244,17 +236,19 @@
             packed[im, side] = jnp.where(low_lane, upper, swap(lower)) if side == 0 else jnp.where(low_lane, swap(upper), lower)
 
     def mine_spectra(p):
-        def step(k, _):
-            i, j = k // SIDE, k % SIDE
+        def step(i, _):
             at = pl.multiple_of(i * N, N)
             if p == 0:
-                block = own[pl.ds(at, N), pl.ds(pl.multiple_of(j * N, N), N)]
+                blocks = [own[pl.ds(at, N), j * N : j * N + N] for j in range(SIDE)]
             else:
-                block = ext[0, pl.ds(pl.multiple_of(at + HALF, HALF), N), pl.ds(pl.multiple_of(j * N + N, N), N)]
-            spec[9 * p + k] = forward(block, t)
+                at = pl.multiple_of(at + HALF, HALF)
+                blocks = [ext[0, pl.ds(at, N), j * N + N : j * N + 2 * N] for j in range(SIDE)]
+            found = forward(jnp.concatenate(blocks, 0), t)
+            for j in range(SIDE):
+                spec[9 * p + SIDE * i + j] = found[j * N : j * N + N]
             return 0
 
-        lax.fori_loop(0, SIDE * SIDE, step, 0)
+        lax.fori_loop(0, SIDE, step, 0)
 
     mine_spectra(0)
 
@@ -319,6 +313,7 @@
         row = iota((N, N), 0)
         low = lane < HALF
         found = dtile[...]
+        stack = []
         top = HALF + i * N
         for j in range(SIDE):
             def at(rows, block):
@@ -330,17 +325,21 @@
 
             centre = slice(top, top + N)
             above, below = slice(top - HALF, top), slice(top + N, top + N + HALF)
-            dy, dx = off[0, p, i, j], off[1, p, i, j]
+            dy, dx = off[0, i, p, j], off[1, i, p, j]
             in_rows = (row >= dy) & (row < dy + N)
             in_cols = (lane >= dx) & (lane < dx + N)
             main = jnp.where(in_cols, at(centre, j + 1), beside(centre, N))
             over = jnp.concatenate([at(below, j + 1), at(above, j + 1)], 0)
             over_side = jnp.concatenate([beside(below, HALF), beside(above, HALF)], 0)
-            theirs = jnp.where(in_rows, main, jnp.where(in_cols, over, over_side))
-            scores = inverse(cross(spec[9 * p + SIDE * i + j], forward(theirs, t)), t)
-            peaks = peak(scores, dy, dx)
-            for comp, (shift, by) in enumerate(zip(peaks, (dy, dx))):
-                value = (by.astype(F32) + shift) * (1.0 / N)
+            stack.append(jnp.where(in_rows, main, jnp.where(in_cols, over, over_side)))
+        theirs = forward(jnp.concatenate(stack, 0), t)
+        scores = inverse(
+            jnp.concatenate([cross(spec[9 * p + SIDE * i + j], theirs[j * N : j * N + N]) for j in range(SIDE)], 0), t
+        )
+        shifts = [(off[0, i, p, j], off[1, i, p, j]) for j in range(SIDE)]
+        for comp, found_shifts in enumerate(peaks(scores, shifts)):
+            for j in range(SIDE):
+                value = (shifts[j][comp].astype(F32) + found_shifts[j : j + 1]) * (1.0 / N)
                 found = jnp.where((row8 == i) & (lane8 == 16 * (2 * comp + p) + j), value, found)
         dtile[...] = found
 
@@ -401,7 +400,7 @@
         def _(k=k):
             total_copy(k).start()
     for g in range(4):
-        disp_ref[g // 2, g % 2] = (pltpu.roll(found, N - 16 * g, 1) if g else found)[0:SIDE, 0:SIDE]
+        disp_ref[g // 2, :, g % 2] = (pltpu.roll(found, N - 16 * g, 1) if g else found)[0:SIDE, 0:SIDE]
 
     lane16 = iota((16, N), 1) & 15
 
@@ -491,21 +490,24 @@
         )
     v = pltpu.roll(v, 16 - SIDE, 0)
     for g in range(4):
-        warped_ref[g // 2, g % 2] = pltpu.roll(v, (N - 16 * g - SIDE) % N, 1)[0:SIDE, 0:SIDE]
+        warped_ref[g // 2, :, g % 2] = pltpu.roll(v, (N - 16 * g - SIDE) % N, 1)[0:SIDE, 0:SIDE]
 
 
 def per_device(sizes, images, offsets, warp, stiffness, valid):
     vmem = pl.BlockSpec(memory_space=pltpu.VMEM)
+    anywhere = pl.BlockSpec(memory_space=pl.ANY)
     dma = pltpu.SemaphoreType.DMA
-    out = jax.ShapeDtypeStruct((2, 2, SIDE, SIDE), F32)
+    out = jax.ShapeDtypeStruct((2, SIDE, 2, SIDE), F32)
     n = sizes[0]
-    return pl.pallas_call(
+    turned = (0, 2, 1, 3)
+    outs = pl.pallas_call(
         functools.partial(kernel, sizes),
         name="align",
         out_shape=(out, out),
-        in_specs=[pl.BlockSpec(memory_space=pl.ANY), pl.BlockSpec(memory_space=pltpu.SMEM)] + [vmem] * 11,
+        in_specs=[anywhere, pl.BlockSpec(memory_space=pltpu.SMEM), vmem, vmem, vmem, anywhere],
         out_specs=(vmem, vmem),
         scratch_shapes=[
+            pltpu.VMEM((2 * N, 6 * N), BF),
             pltpu.VMEM((TILE, TILE), F32),
             pltpu.VMEM((2, TILE + 2 * HALF, TILE + 2 * N), F32),
             pltpu.VMEM((18, N, N), F32),
@@ -519,7 +521,7 @@
             pltpu.VMEM((8, N), F32),
             pltpu.VMEM((n, 8, N), F32),
             pltpu.VMEM((3, 16, N), F32),
-            dma((2,)),
+            dma((3,)),
             dma((1,)),
             dma((1,)),
             dma((4,)),
@@ -536,9 +538,17 @@
             dma((9,)),
         ],
         compiler_params=pltpu.CompilerParams(
-            collective_id=0, has_side_effects=True, vmem_limit_bytes=32 * 1024 * 1024
+            collective_id=0, has_side_effects=True, vmem_limit_bytes=60 * 1024 * 1024
         ),
-    )(images, offsets, warp, stiffness, valid, *(jnp.asarray(a) for a in tables()))
+    )(
+        images,
+        offsets.transpose(turned),
+        warp.transpose(turned),
+        stiffness.transpose(turned),
+        valid.transpose(1, 0, 2),
+        jnp.asarray(tables()),
+    )
+    return tuple(x.transpose(turned) for x in outs)
 
 
 def solution(mesh):

time: 99.3 us -> 82.8 us (0.83)
  local copies, waits for them, and re-layouts: 12.1 us -> 2.57 us
  Pallas kernels: 85.9 us -> 79.4 us
    unnamed x22 -> x2, local copies, waits for them, and re-layouts: 10.9 us -> 2.57 us
    pallas_call x1, Pallas kernels: 85.9 us -> 79.4 us  [per_device(): pl.pallas_call(functools.partial(kernel, sizes), name='align', out_shape=...]
    pallas_call x2 -> x0, local copies, waits for them, and re-layouts: 1.19 us -> none  [per_device(): pl.pallas_call(functools.partial(kernel, sizes), name='align', out_shape=...]
where the time goes in v2:
time: 82.8 us; the launch traced here: 82.6 us
  Pallas kernels  79.4 us (96%)
  local copies, waits for them, and re-layouts  2.57 us (3%)
    pallas_call x1, Pallas kernels, per_device(): pl.pallas_call(functools.partial(kernel, sizes), name='align', out_shape=...  79.4 us
    unnamed x2, local copies, waits for them, and re-layouts  2.57 us

profile of v2, /device:TPU:30, one launch (start us, length us, event | category | flops | bytes accessed | tf_op | source)
XLA Modules:
  0.0 82.6 jit_solution(14838246951465084248)
XLA Ops:
  0.6 79.4 %align.1 = (f32[2,3,2,3]{3,2,1,0:T(2,128)}, f32[2,3,2,3]{3,2,1,0:T(2,128)}) custom-call(f32[2,384,384]{2,1,0:T(8,128)} %images.1, s32[2,3,2,3]{3,2,1,0:T(2,128)} %bitcast.6, f32[2,3,2,3]{3,2,1,0:T(2,128)} %bitcast.7, f32[2,3,2,3]{3,2,1,0:T(2,128)} %bitcast.8, s32[3,2,3]{2,1,0:T(2,128)} %bitcast.11, bf16[256,768]{1,0:T(8,128)(2,1)} %constant.2.clone.table), custom_call_target="tpu_custom_call" | custom-call | tf_op jit(solution)/shard_map/align/pallas_call | solution.py:503
  80.0 1.3 %copy.10 = f32[2,2,3,3]{3,1,2,0:T(2,128)} copy(f32[2,2,3,3]{3,1,2,0:T(2,128)} %bitcast.10) | data formatting | bytes 288
  81.3 1.3 %copy.11 = f32[2,2,3,3]{3,1,2,0:T(2,128)} copy(f32[2,2,3,3]{3,1,2,0:T(2,128)} %bitcast.9) | data formatting | bytes 288

commit v3 on v2

--- a/solution.py
+++ b/solution.py
@@ -18,6 +18,8 @@
 SHARPNESS = 80.0
 ANCHOR = 0.2
 ITERS = 3
+LEGS = 4
+PARTS = (2, 4)
 BF = jnp.bfloat16
 F32 = jnp.float32
 
@@ -124,10 +126,14 @@
 
 
 def kernel(sizes, images, off, warp, stiff, valid, table, disp_ref, warped_ref, *rest):
-    (t, own, ext, spec, packed, landed, small, ptile, pslots, ttile, tslots, dtile, dslots, strips) = rest[:14]
-    lsem, ts, tr, rs, rr, cs, cr, ks, kr, ps, pr, ds, dr, ns, nr = rest[14:]
+    (t, own, ext, spec, packed, landed, transit, small, ftile, fslots, dtile, dslots, strips) = rest[:13]
+    lsem, ts, tr, rs, rr, cs, cr, ks, kr, ds, dr, fs, fr = rest[13:]
     ns_, nr_, nc_ = sizes
+    ny_, nz_ = nr_ // 2, 2 * nc_
+    hop = nc_ // LEGS
     s, r, c = lax.axis_index("sec"), lax.axis_index("row"), lax.axis_index("col")
+    y, half = r // 2, lax.rem(r, 2)
+    z = half * nc_ + c
 
     def inside(a, b, e):
         ok = None
@@ -140,6 +146,13 @@
     def there(a, b, e):
         return (s + a, r + b, c + e)
 
+    def on_line(a, to_y, to_z):
+        to_z = lax.rem(to_z + 2 * nz_, nz_)
+        return (s + a, 2 * to_y + to_z // nc_, lax.rem(to_z, nc_))
+
+    def half_at(at_z):
+        return lax.rem(at_z + 2 * nz_, nz_) // nc_
+
     locals_ = [
         pltpu.make_async_copy(images.at[0], own, lsem.at[0]),
         pltpu.make_async_copy(images.at[1], ext.at[0, HALF : HALF + TILE, N : N + TILE], lsem.at[1]),
@@ -148,10 +161,8 @@
     for copy in locals_:
         copy.start()
 
-    near = [(a, b) for a in (-1, 0, 1) for b in (-1, 0, 1) if (a, b) != (0, 0)]
-    sides = [(-1, 0), (1, 0), (0, -1), (0, 1)]
-    goes = [(k, 0, 0) for k in range(1, ns_)] + [(-1, 0, 0)] + [(-1, b, e) for b, e in sides] + [(0, b, e) for b, e in near]
     barrier = pltpu.get_barrier_semaphore()
+    goes = [(k, 0, 0) for k in range(1, ns_)] + [(-1, 0, 0), (-1, 0, -1), (-1, 0, 1), (0, 0, -1), (0, 0, 1)]
     expected = 0
     for a, b, e in goes:
         @pl.when(inside(-a, -b, -e))
@@ -159,6 +170,16 @@
             pl.semaphore_signal(barrier, inc=1, device_id=there(-a, -b, -e), device_id_type=MESH)
 
         expected = expected + inside(a, b, e).astype(jnp.int32)
+    for a, e in ((0, hop), (0, -hop), (-1, -hop)):
+        for b in (-1, 0, 1):
+            def both(sign, a=a, b=b):
+                return (s + sign * a >= 0) & (s + sign * a < ns_) & (y + sign * b >= 0) & (y + sign * b < ny_)
+
+            @pl.when(both(-1))
+            def _(a=a, b=b, e=e):
+                pl.semaphore_signal(barrier, inc=1, device_id=on_line(-a, y - b, z - e), device_id_type=MESH)
+
+            expected = expected + both(1).astype(jnp.int32)
 
     @pl.when(r == 0)
     def _():
@@ -189,12 +210,12 @@
         ext[1] = jnp.zeros((TILE + 2 * HALF, TILE + 2 * N), F32)
         landed[1] = jnp.zeros((2, TILE // 2, N), F32)
 
+    near = [(b, e) for b in (-1, 0, 1) for e in (-1, 0, 1) if (b, e) != (0, 0)]
     blank = jnp.zeros((8, N), F32)
     for b, e in near:
         @pl.when(jnp.logical_not(inside(0, b, e)))
         def _(b=b, e=e):
-            pslots[3 * (b + 1) + e + 1] = blank
-            tslots[3 * (b + 1) + e + 1] = blank
+            fslots[3 * (b + 1) + e + 1] = blank
 
     for k in range(ns_):
         @pl.when(s <= k)
@@ -220,7 +241,6 @@
         for q, quantity in enumerate((w, right, down, small[8 + sec])):
             by = 16 * g + SIDE * q
             held = held + (pltpu.roll(quantity, by, 1) if by else quantity)
-    ptile[...] = held
 
     for copy in locals_:
         copy.wait()
@@ -265,125 +285,203 @@
             packed.at[1 - p, side], landed.at[p, 1 - side], cs.at[2 * p + side], cr.at[2 * p + 1 - side], there(-p, 0, e)
         )
 
-    def row_rim(p, side):
-        b = 2 * side - 1
-        src = images.at[1 - p, TILE - HALF : TILE, :] if side else images.at[1 - p, 0:HALF, :]
-        at = slice(0, HALF) if side else slice(HALF + TILE, 2 * HALF + TILE)
-        return remote(src, ext.at[p, at, N : N + TILE], rs.at[2 * p + side], rr.at[2 * p + 1 - side], there(-p, b, 0))
-
-    def corner(p, end, side):
-        e = 2 * side - 1
-        at = slice(HALF + TILE, 2 * HALF + TILE) if end else slice(0, HALF)
+    def tile_copy():
+        return remote(images.at[0], ext.at[1, HALF : HALF + TILE, N : N + TILE], ts.at[0], tr.at[0], there(-1, 0, 0))
+
+    turn_y = 2 * half - 1
+    has_cross = (y + turn_y >= 0) & (y + turn_y < ny_)
+    first_at, last_at = 0, HALF + TILE
+
+    def takes(at_y):
+        return ny_ - 1 - at_y
+
+    def rows_of(kind):
+        return HALF // PARTS[kind]
+
+    def rim_at(kind, of_half):
+        return of_half * last_at if kind else (1 - of_half) * last_at
+
+    def leg(p, kind, k, m):
+        sign = 1 - 2 * p
+        n = rows_of(kind)
+        index = ((p * 2 + kind) * LEGS + k) * PARTS[1] + m
+        if k == 0:
+            top = pl.multiple_of((half if kind else 1 - half) * (TILE - HALF) + m * n, 8)
+            src = images.at[1 - p, pl.ds(top, n), :]
+            to_y = y
+            if kind:
+                early = ((half == 1) & (m >= takes(y))) | ((half == 0) & (m < takes(y - 1)))
+                to_y = jnp.where(early, y + turn_y, y)
+            target = on_line(-p, to_y, z + sign * hop)
+        else:
+            src = transit.at[p, kind, k - 1, pl.ds(m * n, n), :]
+            to_y = y
+            if kind and k == LEGS - 1:
+                from_half = half_at(z - sign * hop * k)
+                late = ((from_half == 1) & (m < takes(y))) | ((from_half == 0) & (m > takes(y)))
+                to_y = jnp.where(late, y + 2 * from_half - 1, y)
+            target = on_line(0, to_y, z + sign * hop)
+        if k == LEGS - 1:
+            at = pl.multiple_of(rim_at(kind, half_at(z + sign * hop)) + m * n, 8)
+            dst = ext.at[p, pl.ds(at, n), N : N + TILE]
+        else:
+            dst = transit.at[p, kind, k, pl.ds(m * n, n), :]
+        return remote(src, dst, rs.at[index], rr.at[index], target)
+
+    def leg_comes(p, kind, k, m):
+        ok = s + p < ns_
+        if kind:
+            ok = ok & (has_cross if k == LEGS - 1 else m != takes(y))
+        return ok
+
+    def leg_goes(p, kind, k, m):
+        if k:
+            return leg_comes(p, kind, k - 1, m)
+        return (s - p >= 0) & has_cross if kind else s - p >= 0
+
+    def begin(kind, pairs=(0, 1)):
+        for m in range(PARTS[kind]):
+            for p in pairs:
+                @pl.when(leg_goes(p, kind, 0, m))
+                def _(p=p, m=m):
+                    leg(p, kind, 0, m).start()
+
+    def pass_on(kind, k):
+        for m in range(PARTS[kind]):
+            for p in range(2):
+                @pl.when(leg_comes(p, kind, k, m))
+                def _(p=p, m=m):
+                    leg(p, kind, k, m).wait_recv()
+                    if k < LEGS - 1:
+                        leg(p, kind, k + 1, m).start()
+
+    def corner(p, kind, side):
+        at = pl.multiple_of(rim_at(kind, half), 8)
         src = slice(TILE, TILE + N) if side else slice(N, 2 * N)
         dst = slice(0, N) if side else slice(N + TILE, 2 * N + TILE)
-        n = 4 * p + 2 * end
-        return remote(ext.at[p, at, src], ext.at[p, at, dst], ks.at[n + side], kr.at[n + 1 - side], there(0, 0, e))
-
-    def tile_copy():
-        return remote(images.at[0], ext.at[1, HALF : HALF + TILE, N : N + TILE], ts.at[0], tr.at[0], there(-1, 0, 0))
-
-    def frame_copy(src, slots, send, recv, b, e):
+        n = 4 * p + 2 * kind
+        rows = pl.ds(at, HALF)
+        return remote(
+            ext.at[p, rows, src], ext.at[p, rows, dst], ks.at[n + side], kr.at[n + 1 - side], there(0, 0, 2 * side - 1)
+        )
+
+    def corner_moves(p, kind, e):
+        ok = (s + p < ns_) & inside(0, 0, e)
+        return ok & has_cross if kind else ok
+
+    def send_corners(kind):
+        for p in range(2):
+            for side in range(2):
+                @pl.when(corner_moves(p, kind, 2 * side - 1))
+                def _(p=p, side=side):
+                    corner(p, kind, side).start()
+
+    def await_corners(kind, p):
+        for side in range(2):
+            @pl.when(corner_moves(p, kind, 1 - 2 * side))
+            def _(side=side):
+                corner(p, kind, side).wait_recv()
+
+    def frame_copy(b, e):
         n, m = 3 * (b + 1) + e + 1, 3 * (1 - b) + 1 - e
-        return remote(src, slots.at[m], send.at[n], recv.at[m], there(0, b, e))
-
-    for b, e in near:
-        @pl.when(inside(0, b, e))
-        def _(b=b, e=e):
-            frame_copy(ptile, pslots, ps, pr, b, e).start()
-
+        return remote(ftile, fslots.at[m], fs.at[n], fr.at[m], there(0, b, e))
+
+    def match(vertices):
+        lane = iota((N, N), 1)
+        row = iota((N, N), 0)
+        low = lane < HALF
+        found = dtile[...]
+        stack = []
+        for p, i, j in vertices:
+            top = i * N
+
+            def at(first, rows, block):
+                if not isinstance(i, int):
+                    first = pl.multiple_of(first, HALF)
+                return ext[p, pl.ds(first, rows), block * N : block * N + N]
+
+            def beside(first, rows):
+                left, right = at(first, rows, j), at(first, rows, j + 2)
+                return jnp.where(low[:rows], right, left)
+
+            dy, dx = off[0, i, p, j], off[1, i, p, j]
+            in_rows = (row >= dy) & (row < dy + N)
+            in_cols = (lane >= dx) & (lane < dx + N)
+            main = jnp.where(in_cols, at(top + HALF, N, j + 1), beside(top + HALF, N))
+            over = jnp.concatenate([at(top + HALF + N, HALF, j + 1), at(top, HALF, j + 1)], 0)
+            over_side = jnp.concatenate([beside(top + HALF + N, HALF), beside(top, HALF)], 0)
+            stack.append(jnp.where(in_rows, main, jnp.where(in_cols, over, over_side)))
+        theirs = forward(jnp.concatenate(stack, 0), t)
+        scores = inverse(
+            jnp.concatenate(
+                [cross(spec[9 * p + SIDE * i + j], theirs[k * N : k * N + N]) for k, (p, i, j) in enumerate(vertices)], 0
+            ),
+            t,
+        )
+        shifts = [(off[0, i, p, j], off[1, i, p, j]) for p, i, j in vertices]
+        for comp, found_shifts in enumerate(peaks(scores, shifts)):
+            for k, (p, i, j) in enumerate(vertices):
+                value = (shifts[k][comp].astype(F32) + found_shifts[k : k + 1]) * (1.0 / N)
+                found = jnp.where((row8 == i) & (lane8 == 16 * (2 * comp + p) + j), value, found)
+        dtile[...] = found
+
+    def match_row(p, i):
+        match([(p, i, j) for j in range(SIDE)])
+
+    def fill_columns(p):
+        for side in range(2):
+            @pl.when(inside(p, 0, 1 - 2 * side))
+            def _(side=side):
+                col_rim(p, side).wait_recv()
+        for side in range(2):
+            got = landed[p, side]
+            column = slice(0, N) if side == 0 else slice(N + TILE, 2 * N + TILE)
+            turned = swap(got)
+            upper, lower = (turned, got) if side == 0 else (got, turned)
+            ext[p, HALF : HALF + TILE // 2, column] = upper
+            ext[p, HALF + TILE // 2 : HALF + TILE, column] = lower
+
+    dtile[...] = blank
+
+    begin(0)
     for p in (0, 1):
         for side in range(2):
             @pl.when(inside(-p, 0, 2 * side - 1))
             def _(p=p, side=side):
                 col_rim(p, side).start()
-    for p in (1, 0):
-        for side in range(2):
-            @pl.when(inside(-p, 2 * side - 1, 0))
-            def _(p=p, side=side):
-                row_rim(p, side).start()
+    begin(1)
 
     @pl.when(s > 0)
     def _():
         tile_copy().start()
 
     mine_spectra(1)
-
-    def match_row(p, i):
-        lane = iota((N, N), 1)
-        row = iota((N, N), 0)
-        low = lane < HALF
-        found = dtile[...]
-        stack = []
-        top = HALF + i * N
-        for j in range(SIDE):
-            def at(rows, block):
-                return ext[p, rows, block * N : block * N + N]
-
-            def beside(rows, width):
-                left, right = at(rows, j), at(rows, j + 2)
-                return jnp.where(low[:width], right, left)
-
-            centre = slice(top, top + N)
-            above, below = slice(top - HALF, top), slice(top + N, top + N + HALF)
-            dy, dx = off[0, i, p, j], off[1, i, p, j]
-            in_rows = (row >= dy) & (row < dy + N)
-            in_cols = (lane >= dx) & (lane < dx + N)
-            main = jnp.where(in_cols, at(centre, j + 1), beside(centre, N))
-            over = jnp.concatenate([at(below, j + 1), at(above, j + 1)], 0)
-            over_side = jnp.concatenate([beside(below, HALF), beside(above, HALF)], 0)
-            stack.append(jnp.where(in_rows, main, jnp.where(in_cols, over, over_side)))
-        theirs = forward(jnp.concatenate(stack, 0), t)
-        scores = inverse(
-            jnp.concatenate([cross(spec[9 * p + SIDE * i + j], theirs[j * N : j * N + N]) for j in range(SIDE)], 0), t
-        )
-        shifts = [(off[0, i, p, j], off[1, i, p, j]) for j in range(SIDE)]
-        for comp, found_shifts in enumerate(peaks(scores, shifts)):
-            for j in range(SIDE):
-                value = (shifts[j][comp].astype(F32) + found_shifts[j : j + 1]) * (1.0 / N)
-                found = jnp.where((row8 == i) & (lane8 == 16 * (2 * comp + p) + j), value, found)
-        dtile[...] = found
-
-    dtile[...] = blank
-
-    for p in (0, 1):
-        for side in range(2):
-            @pl.when(inside(p, 0, 1 - 2 * side))
-            def _(p=p, side=side):
-                col_rim(p, side).wait_recv()
-        if p == 1:
+    for k in range(LEGS - 1):
+        pass_on(0, k)
+        pass_on(1, k)
+        if k == 0:
+            fill_columns(0)
+            match_row(0, 1)
+        if k == min(1, LEGS - 2):
             @pl.when(s < ns_ - 1)
             def _():
                 tile_copy().wait_recv()
-        for side in range(2):
-            got = landed[p, side]
-            column = slice(0, N) if side == 0 else slice(N + TILE, 2 * N + TILE)
-            turned = swap(got)
-            if side == 0:
-                upper, lower = turned, got
-            else:
-                upper, lower = got, turned
-            ext[p, HALF : HALF + TILE // 2, column] = upper
-            ext[p, HALF + TILE // 2 : HALF + TILE, column] = lower
-        match_row(p, 1)
-
-    for p in (1, 0):
-        for end in range(2):
-            side = 1 - end
-            @pl.when(inside(p, 1 - 2 * side, 0))
-            def _(p=p, side=side):
-                row_rim(p, side).wait_recv()
-
-            for e in range(2):
-                @pl.when(inside(p, 1 - 2 * side, 0) & inside(0, 0, 2 * e - 1))
-                def _(p=p, end=end, e=e):
-                    corner(p, end, e).start()
-        for end in range(2):
-            side = 1 - end
-            for e in range(2):
-                @pl.when(inside(p, 1 - 2 * side, 0) & inside(0, 0, 1 - 2 * e))
-                def _(p=p, end=end, e=e):
-                    corner(p, end, e).wait_recv()
-            match_row(p, 2 * end)
+
+            fill_columns(1)
+            match_row(1, 1)
+    pass_on(0, LEGS - 1)
+    send_corners(0)
+    along = 2 * (1 - half)
+    for p in range(2):
+        await_corners(0, p)
+        match_row(p, along)
+    pass_on(1, LEGS - 1)
+    send_corners(1)
+    across = 2 * half
+    match([(p, across, 1) for p in range(2)])
+    for p in range(2):
+        await_corners(1, p)
+    match([(p, across, j) for p in range(2) for j in (0, 2)])
 
     silent = (s == ns_ - 1) & ((lane8 & 16) != 0)
     found = jnp.where(silent, 0.0, dtile[...])
@@ -401,35 +499,7 @@
             total_copy(k).start()
     for g in range(4):
         disp_ref[g // 2, :, g % 2] = (pltpu.roll(found, N - 16 * g, 1) if g else found)[0:SIDE, 0:SIDE]
-
-    lane16 = iota((16, N), 1) & 15
-
-    def frame(q):
-        out = jnp.zeros((16, N), F32)
-        for e in (-1, 0, 1):
-            at = SIDE * (e + 1)
-            by = (at - SIDE * q) % N
-            strip = strips[e + 1]
-            strip = pltpu.roll(strip, by, 1) if by else strip
-            out = jnp.where((lane16 >= at) & (lane16 < at + SIDE), strip, out)
-        return out
-
-    def fill(centre, slots):
-        for b in (-1, 0, 1):
-            for e in (-1, 0, 1):
-                at = SIDE * (b + 1)
-                tile = centre[...] if (b, e) == (0, 0) else slots[3 * (b + 1) + e + 1]
-                strips[e + 1, at : at + SIDE, :] = tile[0:SIDE]
-
     strips[...] = jnp.zeros_like(strips)
-    for b, e in near:
-        @pl.when(inside(0, b, e))
-        def _(b=b, e=e):
-            frame_copy(ptile, pslots, ps, pr, -b, -e).wait_recv()
-    fill(ptile, pslots)
-    v, right, down, anchor = (frame(q) for q in range(4))
-    right_left = pltpu.roll(right, 1, 1)
-    down_upper = pltpu.roll(down, 1, 0)
 
     for k in range(ns_ - 1):
         @pl.when(k < s)
@@ -441,11 +511,11 @@
     second = (lane8 & 16) != 0
     below = lower + jnp.where(second, pltpu.roll(lower, 16, 1), pltpu.roll(lower, N - 16, 1))
     below = below + jnp.where(second, pltpu.roll(found, 16, 1), 0.0)
-    ttile[...] = start - below
+    ftile[...] = held + pltpu.roll(start - below, 4 * SIDE, 1)
     for b, e in near:
         @pl.when(inside(0, b, e))
         def _(b=b, e=e):
-            frame_copy(ttile, tslots, ns, nr, b, e).start()
+            frame_copy(b, e).start()
 
     for p in (0, 1):
         for side in range(2):
@@ -453,14 +523,17 @@
             def _(p=p, side=side):
                 col_rim(p, side).wait_send()
 
-            @pl.when(inside(-p, 2 * side - 1, 0))
-            def _(p=p, side=side):
-                row_rim(p, side).wait_send()
-
-            for e in range(2):
-                @pl.when(inside(p, 2 * side - 1, 0) & inside(0, 0, 2 * e - 1))
-                def _(p=p, side=side, e=e):
-                    corner(p, side, e).wait_send()
+            for kind in range(2):
+                @pl.when(corner_moves(p, kind, 2 * side - 1))
+                def _(p=p, kind=kind, side=side):
+                    corner(p, kind, side).wait_send()
+
+        for kind in range(2):
+            for k in range(LEGS):
+                for m in range(PARTS[kind]):
+                    @pl.when(leg_goes(p, kind, k, m))
+                    def _(p=p, kind=kind, k=k, m=m):
+                        leg(p, kind, k, m).wait_send()
 
     @pl.when(s > 0)
     def _():
@@ -473,12 +546,29 @@
     for b, e in near:
         @pl.when(inside(0, b, e))
         def _(b=b, e=e):
-            frame_copy(ptile, pslots, ps, pr, b, e).wait_send()
-            frame_copy(ttile, tslots, ns, nr, b, e).wait_send()
-            frame_copy(ttile, tslots, ns, nr, -b, -e).wait_recv()
-
-    fill(ttile, tslots)
-    target = frame(0)
+            frame_copy(b, e).wait_send()
+            frame_copy(-b, -e).wait_recv()
+
+    for b in (-1, 0, 1):
+        for e in (-1, 0, 1):
+            at = SIDE * (b + 1)
+            tile = ftile[...] if (b, e) == (0, 0) else fslots[3 * (b + 1) + e + 1]
+            strips[e + 1, at : at + SIDE, :] = tile[0:SIDE]
+    lane16 = iota((16, N), 1) & 15
+
+    def frame(q):
+        out = jnp.zeros((16, N), F32)
+        for e in (-1, 0, 1):
+            at = SIDE * (e + 1)
+            by = (at - SIDE * q) % N
+            strip = strips[e + 1]
+            strip = pltpu.roll(strip, by, 1) if by else strip
+            out = jnp.where((lane16 >= at) & (lane16 < at + SIDE), strip, out)
+        return out
+
+    v, right, down, anchor, target = (frame(q) for q in range(5))
+    right_left = pltpu.roll(right, 1, 1)
+    down_upper = pltpu.roll(down, 1, 0)
     for _ in range(ITERS):
         v = (
             v
@@ -513,9 +603,8 @@
             pltpu.VMEM((18, N, N), F32),
             pltpu.VMEM((2, 2, TILE // 2, N), F32),
             pltpu.VMEM((2, 2, TILE // 2, N), F32),
+            pltpu.VMEM((2, 2, LEGS - 1, HALF, TILE), F32),
             pltpu.VMEM((10, 8, N), F32),
-            pltpu.VMEM((8, N), F32),
-            pltpu.VMEM((9, 8, N), F32),
             pltpu.VMEM((8, N), F32),
             pltpu.VMEM((9, 8, N), F32),
             pltpu.VMEM((8, N), F32),
@@ -524,14 +613,12 @@
             dma((3,)),
             dma((1,)),
             dma((1,)),
-            dma((4,)),
-            dma((4,)),
+            dma((4 * LEGS * PARTS[1],)),
+            dma((4 * LEGS * PARTS[1],)),
             dma((4,)),
             dma((4,)),
             dma((8,)),
             dma((8,)),
-            dma((9,)),
-            dma((9,)),
             dma((n,)),
             dma((n,)),
             dma((9,)),

time: 82.8 us -> 76.6 us (0.925)
  the two profiles are of different devices: /device:TPU:30 before, /device:TPU:6 now
where the time goes in v3:
time: 76.6 us; the launch traced here: 76.3 us
  Pallas kernels  73.1 us (95%)
  local copies, waits for them, and re-layouts  2.57 us (3%)
    pallas_call x1, Pallas kernels, per_device(): pl.pallas_call(functools.partial(kernel, sizes), name='align', out_shape=...  73.1 us
    unnamed x2, local copies, waits for them, and re-layouts  2.57 us

profile of v3, /device:TPU:6, one launch (start us, length us, event | category | flops | bytes accessed | tf_op | source)
XLA Modules:
  0.0 76.3 jit_solution(8501264668617687690)
XLA Ops:
  0.6 73.1 %align.1 = (f32[2,3,2,3]{3,2,1,0:T(2,128)}, f32[2,3,2,3]{3,2,1,0:T(2,128)}) custom-call(f32[2,384,384]{2,1,0:T(8,128)} %images.1, s32[2,3,2,3]{3,2,1,0:T(2,128)} %bitcast.6, f32[2,3,2,3]{3,2,1,0:T(2,128)} %bitcast.7, f32[2,3,2,3]{3,2,1,0:T(2,128)} %bitcast.8, s32[3,2,3]{2,1,0:T(2,128)} %bitcast.11, bf16[256,768]{1,0:T(8,128)(2,1)} %constant.2.clone.table), custom_call_target="tpu_custom_call" | custom-call | tf_op jit(solution)/shard_map/align/pallas_call | solution.py:593
  73.8 1.3 %copy.10 = f32[2,2,3,3]{3,1,2,0:T(2,128)} copy(f32[2,2,3,3]{3,1,2,0:T(2,128)} %bitcast.10) | data formatting | bytes 288
  75.1 1.3 %copy.11 = f32[2,2,3,3]{3,1,2,0:T(2,128)} copy(f32[2,2,3,3]{3,1,2,0:T(2,128)} %bitcast.9) | data formatting | bytes 288

commit v4 on v3

--- a/solution.py
+++ b/solution.py
@@ -125,9 +125,10 @@
     return sums[1] / sums[0], sums[2] / sums[0]
 
 
-def kernel(sizes, images, off, warp, stiff, valid, table, disp_ref, warped_ref, *rest):
-    (t, own, ext, spec, packed, landed, transit, small, ftile, fslots, dtile, dslots, strips) = rest[:13]
-    lsem, ts, tr, rs, rr, cs, cr, ks, kr, ds, dr, fs, fr = rest[13:]
+def kernel(sizes, images, off_in, warp_in, stiff_in, valid_in, table, out_ref, *rest):
+    (off, warp, stiff, valid, t, own, ext, spec, packed, landed, transit, cpacked, clanded) = rest[:13]
+    (small, ftile, fslots, dtile, dslots, strips) = rest[13:19]
+    lsem, ts, tr, rs, rr, cs, cr, ks, kr, ds, dr, fs, fr = rest[19:]
     ns_, nr_, nc_ = sizes
     ny_, nz_ = nr_ // 2, 2 * nc_
     hop = nc_ // LEGS
@@ -153,14 +154,6 @@
     def half_at(at_z):
         return lax.rem(at_z + 2 * nz_, nz_) // nc_
 
-    locals_ = [
-        pltpu.make_async_copy(images.at[0], own, lsem.at[0]),
-        pltpu.make_async_copy(images.at[1], ext.at[0, HALF : HALF + TILE, N : N + TILE], lsem.at[1]),
-        pltpu.make_async_copy(table, t, lsem.at[2]),
-    ]
-    for copy in locals_:
-        copy.start()
-
     barrier = pltpu.get_barrier_semaphore()
     goes = [(k, 0, 0) for k in range(1, ns_)] + [(-1, 0, 0), (-1, 0, -1), (-1, 0, 1), (0, 0, -1), (0, 0, 1)]
     expected = 0
@@ -181,6 +174,23 @@
 
             expected = expected + both(1).astype(jnp.int32)
 
+    locals_ = [
+        pltpu.make_async_copy(src, dst, lsem.at[k])
+        for k, (src, dst) in enumerate(
+            (
+                (images.at[1], ext.at[0, HALF : HALF + TILE, N : N + TILE]),
+                (images.at[0], own),
+                (table, t),
+                (off_in, off),
+                (warp_in, warp),
+                (stiff_in, stiff),
+                (valid_in, valid),
+            )
+        )
+    ]
+    for copy in locals_:
+        copy.start()
+
     @pl.when(r == 0)
     def _():
         for p in range(2):
@@ -222,38 +232,26 @@
         def _(k=k):
             dslots[k] = blank
 
-    row8, lane8 = iota((8, N), 0), iota((8, N), 1)
-    small[...] = jnp.zeros_like(small)
-    for comp in range(2):
-        for sec in range(2):
-            small[2 * comp + sec, 0:SIDE, 0:SIDE] = warp[comp, :, sec]
-            small[4 + 2 * comp + sec, 0:SIDE, 0:SIDE] = stiff[comp, :, sec]
-    for sec in range(2):
-        small[8 + sec, 0:SIDE, 0:SIDE] = ANCHOR * valid[:, sec].astype(F32)
-    start = jnp.zeros((8, N), F32)
-    held = jnp.zeros((8, N), F32)
-    for g in range(4):
-        sec = g % 2
-        w = small[g]
-        right = jnp.where((c == nc_ - 1) & (lane8 == SIDE - 1), 0.0, small[4 + sec])
-        down = jnp.where((r == nr_ - 1) & (row8 == SIDE - 1), 0.0, small[6 + sec])
-        start = start + (pltpu.roll(w, 16 * g, 1) if g else w)
-        for q, quantity in enumerate((w, right, down, small[8 + sec])):
-            by = 16 * g + SIDE * q
-            held = held + (pltpu.roll(quantity, by, 1) if by else quantity)
-
-    for copy in locals_:
+    for copy in locals_[:2]:
         copy.wait()
 
-    low_lane = iota((TILE // 2, N), 1) < HALF
+    def pack(strip, side):
+        count = strip.shape[0] // 2
+        upper, lower = strip[:count], strip[count:]
+        low = iota((count, N), 1) < HALF
+        return jnp.where(low, swap(upper), lower) if side else jnp.where(low, upper, swap(lower))
+
+    def unpack(got, side):
+        turned = swap(got)
+        return (got, turned) if side else (turned, got)
+
     for im in range(2):
         for side in range(2):
             if im == 0:
                 strip = own[:, 0:N] if side == 0 else own[:, TILE - N :]
             else:
                 strip = ext[0, HALF : HALF + TILE, N : 2 * N] if side == 0 else ext[0, HALF : HALF + TILE, TILE : TILE + N]
-            upper, lower = strip[: TILE // 2], strip[TILE // 2 :]
-            packed[im, side] = jnp.where(low_lane, upper, swap(lower)) if side == 0 else jnp.where(low_lane, swap(upper), lower)
+            packed[im, side] = pack(strip, side)
 
     def mine_spectra(p):
         def step(i, _):
@@ -270,8 +268,6 @@
 
         lax.fori_loop(0, SIDE, step, 0)
 
-    mine_spectra(0)
-
     pl.semaphore_wait(barrier, expected)
 
     def remote(src, dst, send, recv, target):
@@ -301,10 +297,12 @@
     def rim_at(kind, of_half):
         return of_half * last_at if kind else (1 - of_half) * last_at
 
-    def leg(p, kind, k, m):
+    def leg(p, kind, k, m, block=None):
         sign = 1 - 2 * p
         n = rows_of(kind)
-        index = ((p * 2 + kind) * LEGS + k) * PARTS[1] + m
+        index = (p * 2 + kind) * PARTS[1] + m
+        index = index * (LEGS - 1) + k if block is None else 4 * PARTS[1] * (LEGS - 1) + index * SIDE + block
+        lanes = slice(0, TILE) if block is None else slice(block * N, block * N + N)
         if k == 0:
             top = pl.multiple_of((half if kind else 1 - half) * (TILE - HALF) + m * n, 8)
             src = images.at[1 - p, pl.ds(top, n), :]
@@ -314,7 +312,7 @@
                 to_y = jnp.where(early, y + turn_y, y)
             target = on_line(-p, to_y, z + sign * hop)
         else:
-            src = transit.at[p, kind, k - 1, pl.ds(m * n, n), :]
+            src = transit.at[p, kind, k - 1, pl.ds(m * n, n), lanes]
             to_y = y
             if kind and k == LEGS - 1:
                 from_half = half_at(z - sign * hop * k)
@@ -323,7 +321,7 @@
             target = on_line(0, to_y, z + sign * hop)
         if k == LEGS - 1:
             at = pl.multiple_of(rim_at(kind, half_at(z + sign * hop)) + m * n, 8)
-            dst = ext.at[p, pl.ds(at, n), N : N + TILE]
+            dst = ext.at[p, pl.ds(at, n), lanes.start + N : lanes.stop + N]
         else:
             dst = transit.at[p, kind, k, pl.ds(m * n, n), :]
         return remote(src, dst, rs.at[index], rr.at[index], target)
@@ -346,24 +344,45 @@
                 def _(p=p, m=m):
                     leg(p, kind, 0, m).start()
 
-    def pass_on(kind, k):
+    def each_part(kind, condition, k, act):
         for m in range(PARTS[kind]):
             for p in range(2):
-                @pl.when(leg_comes(p, kind, k, m))
+                @pl.when(condition(p, kind, k, m))
                 def _(p=p, m=m):
-                    leg(p, kind, k, m).wait_recv()
-                    if k < LEGS - 1:
-                        leg(p, kind, k + 1, m).start()
+                    act(p, m)
+
+    def pass_on(kind, k):
+        def act(p, m):
+            leg(p, kind, k, m).wait_recv()
+            if k < LEGS - 2:
+                leg(p, kind, k + 1, m).start()
+            else:
+                leg(p, kind, k + 1, m, 0).start()
+                leg(p, kind, k + 1, m, SIDE - 1).start()
+
+        each_part(kind, leg_comes, k, act)
+        if k == LEGS - 2:
+            each_part(kind, leg_comes, k, lambda p, m: leg(p, kind, k + 1, m, 1).start())
+
+    def arrive(kind, blocks):
+        def act(p, m):
+            for block in blocks:
+                leg(p, kind, LEGS - 1, m, block).wait_recv()
+
+        each_part(kind, leg_comes, LEGS - 1, act)
 
     def corner(p, kind, side):
-        at = pl.multiple_of(rim_at(kind, half), 8)
-        src = slice(TILE, TILE + N) if side else slice(N, 2 * N)
-        dst = slice(0, N) if side else slice(N + TILE, 2 * N + TILE)
         n = 4 * p + 2 * kind
-        rows = pl.ds(at, HALF)
         return remote(
-            ext.at[p, rows, src], ext.at[p, rows, dst], ks.at[n + side], kr.at[n + 1 - side], there(0, 0, 2 * side - 1)
+            cpacked.at[p, kind, side],
+            clanded.at[p, kind, 1 - side],
+            ks.at[n + side],
+            kr.at[n + 1 - side],
+            there(0, 0, 2 * side - 1),
         )
+
+    def rim_rows(kind):
+        return pl.ds(pl.multiple_of(rim_at(kind, half), HALF), HALF)
 
     def corner_moves(p, kind, e):
         ok = (s + p < ns_) & inside(0, 0, e)
@@ -374,6 +393,8 @@
             for side in range(2):
                 @pl.when(corner_moves(p, kind, 2 * side - 1))
                 def _(p=p, side=side):
+                    src = slice(TILE, TILE + N) if side else slice(N, 2 * N)
+                    cpacked[p, kind, side] = pack(ext[p, rim_rows(kind), src], side)
                     corner(p, kind, side).start()
 
     def await_corners(kind, p):
@@ -381,6 +402,8 @@
             @pl.when(corner_moves(p, kind, 1 - 2 * side))
             def _(side=side):
                 corner(p, kind, side).wait_recv()
+                dst = slice(0, N) if side else slice(N + TILE, 2 * N + TILE)
+                ext[p, rim_rows(kind), dst] = jnp.concatenate(unpack(clanded[p, kind, 1 - side], 1 - side), 0)
 
     def frame_copy(b, e):
         n, m = 3 * (b + 1) + e + 1, 3 * (1 - b) + 1 - e
@@ -434,14 +457,10 @@
             def _(side=side):
                 col_rim(p, side).wait_recv()
         for side in range(2):
-            got = landed[p, side]
             column = slice(0, N) if side == 0 else slice(N + TILE, 2 * N + TILE)
-            turned = swap(got)
-            upper, lower = (turned, got) if side == 0 else (got, turned)
+            upper, lower = unpack(landed[p, side], side)
             ext[p, HALF : HALF + TILE // 2, column] = upper
             ext[p, HALF + TILE // 2 : HALF + TILE, column] = lower
-
-    dtile[...] = blank
 
     begin(0)
     for p in (0, 1):
@@ -455,33 +474,61 @@
     def _():
         tile_copy().start()
 
+    for copy in locals_[2:]:
+        copy.wait()
+    mine_spectra(0)
+    pass_on(0, 0)
+    pass_on(1, 0)
+    row8, lane8 = iota((8, N), 0), iota((8, N), 1)
+    small[...] = jnp.zeros_like(small)
+    for comp in range(2):
+        for sec in range(2):
+            small[2 * comp + sec, 0:SIDE, 0:SIDE] = warp[comp, :, sec]
+            small[4 + 2 * comp + sec, 0:SIDE, 0:SIDE] = stiff[comp, :, sec]
+    for sec in range(2):
+        small[8 + sec, 0:SIDE, 0:SIDE] = ANCHOR * valid[:, sec].astype(F32)
+    dtile[...] = blank
+    start = jnp.zeros((8, N), F32)
+    held = jnp.zeros((8, N), F32)
+    for g in range(4):
+        sec = g % 2
+        w = small[g]
+        right = jnp.where((c == nc_ - 1) & (lane8 == SIDE - 1), 0.0, small[4 + sec])
+        down = jnp.where((r == nr_ - 1) & (row8 == SIDE - 1), 0.0, small[6 + sec])
+        start = start + (pltpu.roll(w, 16 * g, 1) if g else w)
+        for q, quantity in enumerate((w, right, down, small[8 + sec])):
+            by = 16 * g + SIDE * q
+            held = held + (pltpu.roll(quantity, by, 1) if by else quantity)
+
     mine_spectra(1)
-    for k in range(LEGS - 1):
+    fill_columns(0)
+    for k in range(1, LEGS - 1):
         pass_on(0, k)
         pass_on(1, k)
-        if k == 0:
-            fill_columns(0)
+        if k == 1:
             match_row(0, 1)
-        if k == min(1, LEGS - 2):
-            @pl.when(s < ns_ - 1)
-            def _():
-                tile_copy().wait_recv()
-
-            fill_columns(1)
-            match_row(1, 1)
-    pass_on(0, LEGS - 1)
+    if LEGS < 3:
+        match_row(0, 1)
+
+    @pl.when(s < ns_ - 1)
+    def _():
+        tile_copy().wait_recv()
+
+    fill_columns(1)
+    match_row(1, 1)
+    along, across = 2 * (1 - half), 2 * half
+    arrive(0, (0, SIDE - 1))
     send_corners(0)
-    along = 2 * (1 - half)
-    for p in range(2):
-        await_corners(0, p)
-        match_row(p, along)
-    pass_on(1, LEGS - 1)
+    arrive(0, (1,))
+    match([(p, along, 1) for p in range(2)])
+    arrive(1, (0, SIDE - 1))
     send_corners(1)
-    across = 2 * half
+    arrive(1, (1,))
     match([(p, across, 1) for p in range(2)])
-    for p in range(2):
-        await_corners(1, p)
-    match([(p, across, j) for p in range(2) for j in (0, 2)])
+    for kind, i in ((0, along), (1, across)):
+        for p in range(2):
+            await_corners(kind, p)
+        match([(p, i, j) for p in range(2) for j in (0, 2)])
 
     silent = (s == ns_ - 1) & ((lane8 & 16) != 0)
     found = jnp.where(silent, 0.0, dtile[...])
@@ -498,7 +545,7 @@
         def _(k=k):
             total_copy(k).start()
     for g in range(4):
-        disp_ref[g // 2, :, g % 2] = (pltpu.roll(found, N - 16 * g, 1) if g else found)[0:SIDE, 0:SIDE]
+        out_ref[0, g // 2, :, g % 2] = (pltpu.roll(found, N - 16 * g, 1) if g else found)[0:SIDE, 0:SIDE]
     strips[...] = jnp.zeros_like(strips)
 
     for k in range(ns_ - 1):
@@ -533,7 +580,8 @@
                 for m in range(PARTS[kind]):
                     @pl.when(leg_goes(p, kind, k, m))
                     def _(p=p, kind=kind, k=k, m=m):
-                        leg(p, kind, k, m).wait_send()
+                        for block in range(SIDE) if k == LEGS - 1 else (None,):
+                            leg(p, kind, k, m, block).wait_send()
 
     @pl.when(s > 0)
     def _():
@@ -580,23 +628,27 @@
         )
     v = pltpu.roll(v, 16 - SIDE, 0)
     for g in range(4):
-        warped_ref[g // 2, :, g % 2] = pltpu.roll(v, (N - 16 * g - SIDE) % N, 1)[0:SIDE, 0:SIDE]
+        out_ref[1, g // 2, :, g % 2] = pltpu.roll(v, (N - 16 * g - SIDE) % N, 1)[0:SIDE, 0:SIDE]
 
 
 def per_device(sizes, images, offsets, warp, stiffness, valid):
     vmem = pl.BlockSpec(memory_space=pltpu.VMEM)
     anywhere = pl.BlockSpec(memory_space=pl.ANY)
     dma = pltpu.SemaphoreType.DMA
-    out = jax.ShapeDtypeStruct((2, SIDE, 2, SIDE), F32)
+    out = jax.ShapeDtypeStruct((2, 2, SIDE, 2, SIDE), F32)
     n = sizes[0]
     turned = (0, 2, 1, 3)
     outs = pl.pallas_call(
         functools.partial(kernel, sizes),
         name="align",
-        out_shape=(out, out),
-        in_specs=[anywhere, pl.BlockSpec(memory_space=pltpu.SMEM), vmem, vmem, vmem, anywhere],
-        out_specs=(vmem, vmem),
+        out_shape=out,
+        in_specs=[anywhere] * 6,
+        out_specs=vmem,
         scratch_shapes=[
+            pltpu.SMEM((2, SIDE, 2, SIDE), jnp.int32),
+            pltpu.VMEM((2, SIDE, 2, SIDE), F32),
+            pltpu.VMEM((2, SIDE, 2, SIDE), F32),
+            pltpu.VMEM((SIDE, 2, SIDE), jnp.int32),
             pltpu.VMEM((2 * N, 6 * N), BF),
             pltpu.VMEM((TILE, TILE), F32),
             pltpu.VMEM((2, TILE + 2 * HALF, TILE + 2 * N), F32),
@@ -604,17 +656,19 @@
             pltpu.VMEM((2, 2, TILE // 2, N), F32),
             pltpu.VMEM((2, 2, TILE // 2, N), F32),
             pltpu.VMEM((2, 2, LEGS - 1, HALF, TILE), F32),
+            pltpu.VMEM((2, 2, 2, HALF // 2, N), F32),
+            pltpu.VMEM((2, 2, 2, HALF // 2, N), F32),
             pltpu.VMEM((10, 8, N), F32),
             pltpu.VMEM((8, N), F32),
             pltpu.VMEM((9, 8, N), F32),
             pltpu.VMEM((8, N), F32),
             pltpu.VMEM((n, 8, N), F32),
             pltpu.VMEM((3, 16, N), F32),
-            dma((3,)),
+            dma((7,)),
             dma((1,)),
             dma((1,)),
-            dma((4 * LEGS * PARTS[1],)),
-            dma((4 * LEGS * PARTS[1],)),
+            dma((4 * PARTS[1] * (LEGS + 2),)),
+            dma((4 * PARTS[1] * (LEGS + 2),)),
             dma((4,)),
             dma((4,)),
             dma((8,)),

time: 76.6 us -> 71.2 us (0.930)
  Pallas kernels: 73.1 us -> 69.1 us
  local copies, waits for them, and re-layouts: 2.57 us -> 1.31 us
    pallas_call x1, Pallas kernels: 73.1 us -> 69.1 us  [per_device(): pl.pallas_call(functools.partial(kernel, sizes), name='align', out_shape=...]
    unnamed x2 -> x0, local copies, waits for them, and re-layouts: 2.57 us -> none
    transpose x0 -> x1, local copies, waits for them, and re-layouts: none -> 1.31 us  [per_device(): return tuple((x.transpose(turned) for x in outs))]
where the time goes in v4:
time: 71.2 us; the launch traced here: 71.1 us
  Pallas kernels  69.1 us (97%)
  local copies, waits for them, and re-layouts  1.31 us (2%)
    pallas_call x1, Pallas kernels, per_device(): pl.pallas_call(functools.partial(kernel, sizes), name='align', out_shape=...  69.1 us

profile of v4, /device:TPU:6, one launch (start us, length us, event | category | flops | bytes accessed | tf_op | source)
XLA Modules:
  0.0 71.1 jit_solution(3431938871983838847)
XLA Ops:
  0.6 69.1 %align.1 = f32[2,2,3,2,3]{4,3,2,1,0:T(2,128)} custom-call(f32[2,384,384]{2,1,0:T(8,128)} %images.1, s32[2,3,2,3]{3,2,1,0:T(2,128)} %bitcast.12, f32[2,3,2,3]{3,2,1,0:T(2,128)} %bitcast.13, f32[2,3,2,3]{3,2,1,0:T(2,128)} %bitcast.14, s32[3,2,3]{2,1,0:T(2,128)} %bitcast.15, bf16[256,768]{1,0:T(8,128)(2,1)} %constant.2.clone.table), custom_call_target="tpu_custom_call" | custom-call | tf_op jit(solution)/shard_map/align/pallas_call | solution.py:641
  69.8 1.3 %slice_bitcast_fusion = (f32[2,2,3,3]{3,1,2,0:T(2,128)}, f32[2,2,3,3]{3,1,2,0:T(2,128)}) fusion(f32[2,2,3,2,3]{4,3,2,1,0:T(2,128)} %align.1), kind=kLoop, calls=%fused_computation | loop fusion | bytes 576 | tf_op jit(solution)/shard_map/transpose | solution.py:692

commit v5 on v4

--- a/solution.py
+++ b/solution.py
@@ -19,7 +19,7 @@
 ANCHOR = 0.2
 ITERS = 3
 LEGS = 4
-PARTS = (2, 4)
+PARTS = (4, 4)
 BF = jnp.bfloat16
 F32 = jnp.float32
 
@@ -157,22 +157,22 @@
     barrier = pltpu.get_barrier_semaphore()
     goes = [(k, 0, 0) for k in range(1, ns_)] + [(-1, 0, 0), (-1, 0, -1), (-1, 0, 1), (0, 0, -1), (0, 0, 1)]
     expected = 0
+    for a, e in ((0, hop), (0, -hop), (-1, -hop)):
+        for b in (-1, 0, 1):
+            def both(sign, a=a, b=b):
+                return (s + sign * a >= 0) & (s + sign * a < ns_) & (y + sign * b >= 0) & (y + sign * b < ny_)
+
+            @pl.when(both(-1))
+            def _(a=a, b=b, e=e):
+                pl.semaphore_signal(barrier, inc=1, device_id=on_line(-a, y - b, z - e), device_id_type=MESH)
+
+            expected = expected + both(1).astype(jnp.int32)
     for a, b, e in goes:
         @pl.when(inside(-a, -b, -e))
         def _(a=a, b=b, e=e):
             pl.semaphore_signal(barrier, inc=1, device_id=there(-a, -b, -e), device_id_type=MESH)
 
         expected = expected + inside(a, b, e).astype(jnp.int32)
-    for a, e in ((0, hop), (0, -hop), (-1, -hop)):
-        for b in (-1, 0, 1):
-            def both(sign, a=a, b=b):
-                return (s + sign * a >= 0) & (s + sign * a < ns_) & (y + sign * b >= 0) & (y + sign * b < ny_)
-
-            @pl.when(both(-1))
-            def _(a=a, b=b, e=e):
-                pl.semaphore_signal(barrier, inc=1, device_id=on_line(-a, y - b, z - e), device_id_type=MESH)
-
-            expected = expected + both(1).astype(jnp.int32)
 
     locals_ = [
         pltpu.make_async_copy(src, dst, lsem.at[k])
@@ -220,7 +220,7 @@
         ext[1] = jnp.zeros((TILE + 2 * HALF, TILE + 2 * N), F32)
         landed[1] = jnp.zeros((2, TILE // 2, N), F32)
 
-    near = [(b, e) for b in (-1, 0, 1) for e in (-1, 0, 1) if (b, e) != (0, 0)]
+    near = [(b, e) for b in (1, -1, 0) for e in (0, -1, 1) if (b, e) != (0, 0)]
     blank = jnp.zeros((8, N), F32)
     for b, e in near:
         @pl.when(jnp.logical_not(inside(0, b, e)))
@@ -232,9 +232,6 @@
         def _(k=k):
             dslots[k] = blank
 
-    for copy in locals_[:2]:
-        copy.wait()
-
     def pack(strip, side):
         count = strip.shape[0] // 2
         upper, lower = strip[:count], strip[count:]
@@ -244,14 +241,6 @@
     def unpack(got, side):
         turned = swap(got)
         return (got, turned) if side else (turned, got)
-
-    for im in range(2):
-        for side in range(2):
-            if im == 0:
-                strip = own[:, 0:N] if side == 0 else own[:, TILE - N :]
-            else:
-                strip = ext[0, HALF : HALF + TILE, N : 2 * N] if side == 0 else ext[0, HALF : HALF + TILE, TILE : TILE + N]
-            packed[im, side] = pack(strip, side)
 
     def mine_spectra(p):
         def step(i, _):
@@ -463,16 +452,26 @@
             ext[p, HALF + TILE // 2 : HALF + TILE, column] = lower
 
     begin(0)
+    begin(1)
+
+    @pl.when(s > 0)
+    def _():
+        tile_copy().start()
+
+    for copy in locals_[:2]:
+        copy.wait()
+    for im in range(2):
+        for side in range(2):
+            if im == 0:
+                strip = own[:, 0:N] if side == 0 else own[:, TILE - N :]
+            else:
+                strip = ext[0, HALF : HALF + TILE, N : 2 * N] if side == 0 else ext[0, HALF : HALF + TILE, TILE : TILE + N]
+            packed[im, side] = pack(strip, side)
     for p in (0, 1):
         for side in range(2):
             @pl.when(inside(-p, 0, 2 * side - 1))
             def _(p=p, side=side):
                 col_rim(p, side).start()
-    begin(1)
-
-    @pl.when(s > 0)
-    def _():
-        tile_copy().start()
 
     for copy in locals_[2:]:
         copy.wait()
@@ -524,11 +523,12 @@
     arrive(1, (0, SIDE - 1))
     send_corners(1)
     arrive(1, (1,))
-    match([(p, across, 1) for p in range(2)])
-    for kind, i in ((0, along), (1, across)):
-        for p in range(2):
-            await_corners(kind, p)
-        match([(p, i, j) for p in range(2) for j in (0, 2)])
+    for p in range(2):
+        await_corners(0, p)
+    match([(p, across, 1) for p in range(2)] + [(p, along, j) for p in range(2) for j in (0, 2)])
+    for p in range(2):
+        await_corners(1, p)
+    match([(p, across, j) for p in range(2) for j in (0, 2)])
 
     silent = (s == ns_ - 1) & ((lane8 & 16) != 0)
     found = jnp.where(silent, 0.0, dtile[...])

time: 71.2 us -> 70.6 us (level)
    pallas_call x1, Pallas kernels: 69.1 us -> 68.4 us  [per_device(): pl.pallas_call(functools.partial(kernel, sizes), name='align', out_shape=...]
where the time goes in v5:
time: 70.6 us; the launch traced here: 70.3 us
  Pallas kernels  68.4 us (97%)
  local copies, waits for them, and re-layouts  1.31 us (2%)
    pallas_call x1, Pallas kernels, per_device(): pl.pallas_call(functools.partial(kernel, sizes), name='align', out_shape=...  68.4 us

profile of v5, /device:TPU:6, one launch (start us, length us, event | category | flops | bytes accessed | tf_op | source)
XLA Modules:
  0.0 70.3 jit_solution(4010964509583714633)
XLA Ops:
  0.6 68.4 %align.1 = f32[2,2,3,2,3]{4,3,2,1,0:T(2,128)} custom-call(f32[2,384,384]{2,1,0:T(8,128)} %images.1, s32[2,3,2,3]{3,2,1,0:T(2,128)} %bitcast.12, f32[2,3,2,3]{3,2,1,0:T(2,128)} %bitcast.13, f32[2,3,2,3]{3,2,1,0:T(2,128)} %bitcast.14, s32[3,2,3]{2,1,0:T(2,128)} %bitcast.15, bf16[256,768]{1,0:T(8,128)(2,1)} %constant.2.clone.table), custom_call_target="tpu_custom_call" | custom-call | tf_op jit(solution)/shard_map/align/pallas_call | solution.py:641
  69.0 1.3 %slice_bitcast_fusion = (f32[2,2,3,3]{3,1,2,0:T(2,128)}, f32[2,2,3,3]{3,1,2,0:T(2,128)}) fusion(f32[2,2,3,2,3]{4,3,2,1,0:T(2,128)} %align.1), kind=kLoop, calls=%fused_computation | loop fusion | bytes 576 | tf_op jit(solution)/shard_map/transpose | solution.py:692

commit v6 on v5

--- a/solution.py
+++ b/solution.py
@@ -123,6 +123,23 @@
         sums.append((by_col, jnp.sum(weights * rows, axis=0, keepdims=True), by_col * cols))
     sums = [jnp.sum(jnp.concatenate([x[q] for x in sums], 0), axis=1, keepdims=True) for q in range(3)]
     return sums[1] / sums[0], sums[2] / sums[0]
+
+
+class Remote:
+    def __init__(self, src, dst, send, recv, target, here):
+        self.refs, self.target, self.here = (src, dst, send, recv), target, here
+
+    def to(self, device):
+        return pltpu.make_async_remote_copy(*self.refs, device_id=device, device_id_type=MESH)
+
+    def start(self):
+        self.to(self.target).start()
+
+    def wait_recv(self):
+        self.to(self.here).wait_recv()
+
+    def wait_send(self):
+        self.to(self.here).wait_send()
 
 
 def kernel(sizes, images, off_in, warp_in, stiff_in, valid_in, table, out_ref, *rest):
@@ -260,9 +277,7 @@
     pl.semaphore_wait(barrier, expected)
 
     def remote(src, dst, send, recv, target):
-        return pltpu.make_async_remote_copy(
-            src_ref=src, dst_ref=dst, send_sem=send, recv_sem=recv, device_id=target, device_id_type=MESH
-        )
+        return Remote(src, dst, send, recv, target, (s, r, c))
 
     def col_rim(p, side):
         e = 2 * side - 1

time: 70.6 us -> 70.6 us (level)
  no operation moved by 1% of the time
where the time goes in v6:
time: 70.6 us; the launch traced here: 70.3 us
  Pallas kernels  68.4 us (97%)
  local copies, waits for them, and re-layouts  1.31 us (2%)
    pallas_call x1, Pallas kernels, per_device(): pl.pallas_call(functools.partial(kernel, sizes), name='align', out_shape=...  68.4 us

profile of v6, /device:TPU:6, one launch (start us, length us, event | category | flops | bytes accessed | tf_op | source)
XLA Modules:
  0.0 70.3 jit_solution(4010964509583714633)
XLA Ops:
  0.6 68.4 %align.1 = f32[2,2,3,2,3]{4,3,2,1,0:T(2,128)} custom-call(f32[2,384,384]{2,1,0:T(8,128)} %images.1, s32[2,3,2,3]{3,2,1,0:T(2,128)} %bitcast.12, f32[2,3,2,3]{3,2,1,0:T(2,128)} %bitcast.13, f32[2,3,2,3]{3,2,1,0:T(2,128)} %bitcast.14, s32[3,2,3]{2,1,0:T(2,128)} %bitcast.15, bf16[256,768]{1,0:T(8,128)(2,1)} %constant.2.clone.table), custom_call_target="tpu_custom_call" | custom-call | tf_op jit(solution)/shard_map/align/pallas_call | solution.py:656
  69.0 1.3 %slice_bitcast_fusion = (f32[2,2,3,3]{3,1,2,0:T(2,128)}, f32[2,2,3,3]{3,1,2,0:T(2,128)}) fusion(f32[2,2,3,2,3]{4,3,2,1,0:T(2,128)} %align.1), kind=kLoop, calls=%fused_computation | loop fusion | bytes 576 | tf_op jit(solution)/shard_map/transpose | solution.py:707

commit v7 on v6

--- a/solution.py
+++ b/solution.py
@@ -411,7 +411,7 @@
 
     def frame_copy(b, e):
         n, m = 3 * (b + 1) + e + 1, 3 * (1 - b) + 1 - e
-        return remote(ftile, fslots.at[m], fs.at[n], fr.at[m], there(0, b, e))
+        return remote(ftile.at[0:4], fslots.at[m, 0:4], fs.at[n], fr.at[m], there(0, b, e))
 
     def match(vertices):
         lane = iota((N, N), 1)

time: 70.6 us -> 70.4 us (level)
  no operation moved by 1% of the time
where the time goes in v7:
time: 70.4 us; the launch traced here: 70.3 us
  Pallas kernels  68.3 us (97%)
  local copies, waits for them, and re-layouts  1.31 us (2%)
    pallas_call x1, Pallas kernels, per_device(): pl.pallas_call(functools.partial(kernel, sizes), name='align', out_shape=...  68.3 us

profile of v7, /device:TPU:6, one launch (start us, length us, event | category | flops | bytes accessed | tf_op | source)
XLA Modules:
  0.0 70.3 jit_solution(16867604372357043186)
XLA Ops:
  0.6 68.3 %align.1 = f32[2,2,3,2,3]{4,3,2,1,0:T(2,128)} custom-call(f32[2,384,384]{2,1,0:T(8,128)} %images.1, s32[2,3,2,3]{3,2,1,0:T(2,128)} %bitcast.12, f32[2,3,2,3]{3,2,1,0:T(2,128)} %bitcast.13, f32[2,3,2,3]{3,2,1,0:T(2,128)} %bitcast.14, s32[3,2,3]{2,1,0:T(2,128)} %bitcast.15, bf16[256,768]{1,0:T(8,128)(2,1)} %constant.2.clone.table), custom_call_target="tpu_custom_call" | custom-call | tf_op jit(solution)/shard_map/align/pallas_call | solution.py:656
  69.0 1.3 %slice_bitcast_fusion = (f32[2,2,3,3]{3,1,2,0:T(2,128)}, f32[2,2,3,3]{3,1,2,0:T(2,128)}) fusion(f32[2,2,3,2,3]{4,3,2,1,0:T(2,128)} %align.1), kind=kLoop, calls=%fused_computation | loop fusion | bytes 576 | tf_op jit(solution)/shard_map/transpose | solution.py:707
